TPU v7x, 512 devices: a whole 4x8x8 slice. The times are simulated.
512 devices in a mesh: seq: 64 (over y, x, z_lo), ch: 8 (over z_hi, core).
Axes of the slice: x: 4, y: 8, z: 8 (z_hi: 4, z_lo: 2; z = z_hi * 2 + z_lo), core: 2. Of those that a mesh axis runs over, the one named last changes fastest.
Arguments:
- query_gate: bfloat16 [4096, 8192], P('ch', 'seq'), may hold values from -6 to 6
- key_gate: bfloat16 [4096, 8192], P('ch', 'seq'), may hold values from -6 to 6
- value_in: bfloat16 [4096, 8192], P('ch', 'seq'), may hold values from -6 to 6
- filter_weight: bfloat16 [512, 8192], P(None, 'seq'), may hold values from -6 to 6
- output_grad: bfloat16 [4096, 8192], P('ch', 'seq'), may hold values from -6 to 6
Outputs:
- query_grad: bfloat16 [4096, 8192], P('ch', 'seq')
- key_grad: bfloat16 [4096, 8192], P('ch', 'seq')
- value_grad: bfloat16 [4096, 8192], P('ch', 'seq')
- filter_grad: bfloat16 [512, 8192], P('ch', 'seq')
All inputs are finite; a program needn't handle non-finite values.
Results may differ from a plain program's by a relative error of at most 0.0057.
Values may be sent and summed in bfloat16 or wider, within the bound.
A program may use at most 64 MiB of HBM per device.

v0:
```python
import math

import jax
import jax.numpy as jnp
from jax import lax
from jax.sharding import PartitionSpec as P

FACTOR_A = 128


def contract(form, left_side, right_side):
    return jnp.einsum(form, left_side, right_side, precision=lax.Precision.HIGHEST)


def dft_tables(factor_a, factor_b):
    size_full = factor_a * factor_b
    outer_b = lax.broadcasted_iota(jnp.int32, (factor_b, factor_b // 2), 0)
    inner_b = lax.broadcasted_iota(jnp.int32, (factor_b, factor_b // 2), 1)
    angle_b = 2.0 * math.pi / factor_b * (outer_b * inner_b % factor_b).astype(jnp.float32)
    outer_tw = lax.broadcasted_iota(jnp.int32, (factor_b, factor_a), 0)
    inner_tw = lax.broadcasted_iota(jnp.int32, (factor_b, factor_a), 1)
    angle_tw = 2.0 * math.pi / size_full * (outer_tw * inner_tw % size_full).astype(jnp.float32)
    outer_a = lax.broadcasted_iota(jnp.int32, (factor_a, factor_a), 0)
    inner_a = lax.broadcasted_iota(jnp.int32, (factor_a, factor_a), 1)
    angle_a = 2.0 * math.pi / factor_a * (outer_a * inner_a % factor_a).astype(jnp.float32)
    return (
        jnp.cos(angle_b),
        -jnp.sin(angle_b),
        jnp.cos(angle_tw),
        -jnp.sin(angle_tw),
        jnp.cos(angle_a),
        -jnp.sin(angle_a),
    )


def forward_dft(signal, tables):
    b_real, b_imag, tw_real, tw_imag, a_real, a_imag = tables
    first_real = contract("kb,cba->cka", b_real, signal)
    first_imag = contract("kb,cba->cka", b_imag, signal)
    turned_real = first_real * tw_real - first_imag * tw_imag
    turned_imag = first_real * tw_imag + first_imag * tw_real
    out_real = contract("cka,am->ckm", turned_real, a_real) - contract(
        "cka,am->ckm", turned_imag, a_imag
    )
    out_imag = contract("cka,am->ckm", turned_real, a_imag) + contract(
        "cka,am->ckm", turned_imag, a_real
    )
    return (out_real, out_imag)


def inverse_dft(spec_real, spec_imag, tables):
    b_real, b_imag, tw_real, tw_imag, a_real, a_imag = tables
    size_full = a_real.shape[0] * b_real.shape[0]
    mid_real = contract("ckm,ma->cka", spec_real, a_real) + contract(
        "ckm,ma->cka", spec_imag, a_imag
    )
    mid_imag = contract("ckm,ma->cka", spec_imag, a_real) - contract(
        "ckm,ma->cka", spec_real, a_imag
    )
    untw_real = mid_real * tw_real + mid_imag * tw_imag
    untw_imag = mid_imag * tw_real - mid_real * tw_imag
    result = contract("kb,cka->cba", b_real, untw_real) + contract("kb,cka->cba", b_imag, untw_imag)
    return result * (1.0 / size_full)


def shards(query_gate, key_gate, value_in, filter_weight, output_grad):
    seq_count = lax.axis_size("seq")
    ch_count = lax.axis_size("ch")
    local_ch, tokens_dev = query_gate.shape
    filter_count = filter_weight.shape[0]
    length = tokens_dev * seq_count
    factor_b = 2 * length // FACTOR_A
    half_b = factor_b // 2
    groups = local_ch // seq_count
    per_filter = filter_count // seq_count
    norm_factor = length ** (-0.5)
    tables = dft_tables(FACTOR_A, factor_b)
    gated_in = (key_gate.astype(jnp.float32) * value_in.astype(jnp.float32)).astype(jnp.bfloat16)
    inner_grad = (output_grad.astype(jnp.float32) * query_gate.astype(jnp.float32)).astype(
        jnp.bfloat16
    )
    row_block = filter_count // ch_count
    filter_rows = lax.dynamic_slice_in_dim(
        filter_weight, lax.axis_index("ch") * row_block, row_block, 0
    )
    moved_in, moved_grad, moved_filter = (
        lax.all_to_all(
            gated_in.reshape(groups, seq_count, tokens_dev),
            "seq",
            split_axis=1,
            concat_axis=2,
            tiled=True,
        ),
        lax.all_to_all(
            inner_grad.reshape(groups, seq_count, tokens_dev),
            "seq",
            split_axis=1,
            concat_axis=2,
            tiled=True,
        ),
        lax.all_to_all(
            filter_rows.reshape(-1, seq_count, tokens_dev),
            "seq",
            split_axis=1,
            concat_axis=2,
            tiled=True,
        ),
    )

    def as_signal(moved):
        return moved.reshape(-1, half_b, FACTOR_A).astype(jnp.float32)

    in_real, in_imag = forward_dft(as_signal(moved_in), tables)
    grad_real, grad_imag = forward_dft(as_signal(moved_grad), tables)
    filt_real, filt_imag = forward_dft(as_signal(moved_filter), tables)
    filt_real = filt_real * norm_factor
    filt_imag = filt_imag * norm_factor
    filt_real, filt_imag = (
        lax.all_gather(filt_real, "ch", axis=0, tiled=True),
        lax.all_gather(filt_imag, "ch", axis=0, tiled=True),
    )
    spread = (groups // per_filter, per_filter, factor_b, FACTOR_A)
    in_real = in_real.reshape(spread)
    in_imag = in_imag.reshape(spread)
    grad_real = grad_real.reshape(spread)
    grad_imag = grad_imag.reshape(spread)
    conv_real = (filt_real * in_real - filt_imag * in_imag).reshape(groups, factor_b, FACTOR_A)
    conv_imag = (filt_real * in_imag + filt_imag * in_real).reshape(groups, factor_b, FACTOR_A)
    back_real = (filt_real * grad_real + filt_imag * grad_imag).reshape(groups, factor_b, FACTOR_A)
    back_imag = (filt_real * grad_imag - filt_imag * grad_real).reshape(groups, factor_b, FACTOR_A)
    cross_real = jnp.sum(grad_real * in_real + grad_imag * in_imag, axis=0)
    cross_imag = jnp.sum(grad_imag * in_real - grad_real * in_imag, axis=0)
    conv_out = (
        inverse_dft(conv_real, conv_imag, tables).reshape(groups, 1, length).astype(jnp.bfloat16)
    )
    in_grad = (
        inverse_dft(back_real, back_imag, tables).reshape(groups, 1, length).astype(jnp.bfloat16)
    )
    conv_tokens, grad_tokens = (
        lax.all_to_all(conv_out, "seq", split_axis=2, concat_axis=1, tiled=True),
        lax.all_to_all(in_grad, "seq", split_axis=2, concat_axis=1, tiled=True),
    )
    conv_tokens = conv_tokens.reshape(local_ch, tokens_dev).astype(jnp.float32)
    grad_tokens = grad_tokens.reshape(local_ch, tokens_dev).astype(jnp.float32)
    query_grad = (output_grad.astype(jnp.float32) * conv_tokens).astype(jnp.bfloat16)
    key_grad = (grad_tokens * value_in.astype(jnp.float32)).astype(jnp.bfloat16)
    value_grad = (grad_tokens * key_gate.astype(jnp.float32)).astype(jnp.bfloat16)
    filter_time = (inverse_dft(cross_real, cross_imag, tables) * norm_factor).reshape(
        per_filter, 1, length
    )
    returned = lax.all_to_all(filter_time, "seq", split_axis=2, concat_axis=1, tiled=True).reshape(
        filter_count, tokens_dev
    )
    filter_grad = lax.psum_scatter(returned, "ch", scatter_dimension=0, tiled=True).astype(
        jnp.bfloat16
    )
    return (query_grad, key_grad, value_grad, filter_grad)


def solution(mesh):
    placed = (P("ch", "seq"), P("ch", "seq"), P("ch", "seq"), P(None, "seq"), P("ch", "seq"))
    return jax.shard_map(
        shards,
        mesh=mesh,
        in_specs=placed,
        out_specs=(P("ch", "seq"), P("ch", "seq"), P("ch", "seq"), P("ch", "seq")),
        check_vma=False,
    )
```

profile of v0, /device:TPU:6, one launch (start us, length us, event | category | flops | bytes accessed | tf_op | source)
XLA Modules:
  0.0 374.6 jit_solution(7358010886625242399)
XLA Ops:
  8.7 12.4 %all-to-all-start = ((bf16[1,64,128]{2,0,1:T(2,128)(2,1)}), bf16[1,64,128]{2,0,1:T(2,128)(2,1)S(1)}, u32[]{:S(2)}, u32[]{:S(2)}) async-start(bf16[1,64,128]{2,0,1:T(2,128)(2,1)} %copy.113), calls=%async_computation | async-start | bytes 65536 | tf_op jit(solution)/shard_map/all_to_all | solution.py:101
  25.4 4.4 %all-to-all-done = bf16[1,64,128]{2,0,1:T(2,128)(2,1)S(1)} async-done(((bf16[1,64,128]{2,0,1:T(2,128)(2,1)}), bf16[1,64,128]{2,0,1:T(2,128)(2,1)S(1)}, u32[]{:S(2)}, u32[]{:S(2)}) %all-to-all-start) | async-done | bytes 16416 | tf_op jit(solution)/shard_map/all_to_all | solution.py:101
  29.8 6.8 %all-to-all-start.3 = ((bf16[8,64,128]{2,0,1:T(8,128)(2,1)}), bf16[8,64,128]{2,0,1:T(8,128)(2,1)S(1)}, u32[]{:S(2)}, u32[]{:S(2)}) async-start(bf16[8,64,128]{2,0,1:T(8,128)(2,1)} %copy.131), calls=%async_computation.3 | async-start | bytes 262144 | tf_op jit(solution)/shard_map/all_to_all | solution.py:94
  40.1 19.9 %all-gather = f32[1024,128]{1,0:T(8,128)S(1)} all-gather(f32[128,128]{1,0:T(8,128)S(1)} %fusion.9), channel_id=2, replica_groups=mesh['seq'=64,'ch'=8] {'ch'}, dimensions={0}, use_global_device_ids=true | all-gather | bytes 589824 | tf_op jit(solution)/shard_map/all_gather | solution.py:119
  60.0 16.8 %all-gather.1 = f32[1024,128]{1,0:T(8,128)} all-gather(f32[128,128]{1,0:T(8,128)S(1)} %fusion.8), channel_id=3, replica_groups=mesh['seq'=64,'ch'=8] {'ch'}, dimensions={0}, use_global_device_ids=true | all-gather | bytes 589824 | tf_op jit(solution)/shard_map/all_gather | solution.py:120
  76.8 11.2 %all-to-all-start.1 = ((bf16[8,64,128]{2,0,1:T(8,128)(2,1)}), bf16[8,64,128]{2,0,1:T(8,128)(2,1)S(1)}, u32[]{:S(2)}, u32[]{:S(2)}) async-start(bf16[8,64,128]{2,0,1:T(8,128)(2,1)} %copy.114), calls=%async_computation.1 | async-start | bytes 262144 | tf_op jit(solution)/shard_map/all_to_all | solution.py:87
  92.2 5.2 %all-to-all-done.1 = bf16[8,64,128]{2,0,1:T(8,128)(2,1)S(1)} async-done(((bf16[8,64,128]{2,0,1:T(8,128)(2,1)}), bf16[8,64,128]{2,0,1:T(8,128)(2,1)S(1)}, u32[]{:S(2)}, u32[]{:S(2)}) %all-to-all-start.1) | async-done | bytes 131104 | tf_op jit(solution)/shard_map/all_to_all | solution.py:87
  121.2 3.7 copy.180
  125.4 38.5 %reduce.2 = f32[8192,8]{1,0:T(8,128)} reduce(f32[8192,1,8]{2,1,0:T(1,128)} %bitcast.134, f32[]{:T(128)} %broadcast.254), dimensions={1}, to_apply=%bitcast.118.reduce_sub_computation | reduce | bytes 524292
  163.8 4.5 %reshape.225 = f32[64,1,1024]{2,1,0:T(1,128)} reshape(f32[8192,8]{1,0:T(8,128)} %reduce.2) | data formatting | bytes 524288
  168.3 7.5 %all-to-all-start.5 = ((f32[64,1,1024]{2,1,0:T(1,128)}), f32[64,1,1024]{2,1,0:T(1,128)}, u32[]{:S(2)}, u32[]{:S(2)}) async-start(f32[64,1,1024]{2,1,0:T(1,128)} %reshape.225), calls=%async_computation.5 | async-start | bytes 524288 | tf_op jit(solution)/shard_map/all_to_all | solution.py:151
  175.8 6.8 %copy.144 = bf16[8,1,8192]{0,1,2:T(2,128)(2,1)} copy(bf16[8,1,8192]{2,0,1:T(8,128)(2,1)S(1)} %convert_element_type.236) | data formatting | bytes 262144 | tf_op jit(solution)/shard_map/convert_element_type | solution.py:137
  183.1 45.2 %reduce = bf16[8192,8]{1,0:T(8,128)(2,1)S(1)} reduce(bf16[8192,1,8]{2,1,0:T(2,128)(2,1)} %bitcast.135, bf16[]{:T(256)} %broadcast.252), dimensions={1}, to_apply=%bitcast.116.reduce_sub_computation | reduce | bytes 262146
  228.3 2.9 reshape.223
  234.1 11.3 %all-to-all-start.4 = ((bf16[64,2,512]{2,1,0:T(2,128)(2,1)}), bf16[64,2,512]{2,1,0:T(2,128)(2,1)S(1)}, u32[]{:S(2)}, u32[]{:S(2)}) async-start(bf16[64,2,512]{2,1,0:T(2,128)(2,1)} %reshape.223), calls=%async_computation.4 | async-start | bytes 262144 | tf_op jit(solution)/shard_map/all_to_all | solution.py:141
  247.6 8.6 %reshape.226 = f32[8192,1,8]{2,1,0:T(1,128)} reshape(f32[64,1024]{1,0:T(8,128)S(1)} %reduce.3) | data formatting | bytes 524288
  256.2 7.8 %copy.153 = f32[8,1,8192]{2,0,1:T(8,128)S(1)} copy(f32[8,1,8192]{0,1,2:T(1,128)} %bitcast.137) | data formatting | bytes 524288 | tf_op jit(solution)/shard_map/all_to_all | solution.py:151
  265.8 6.7 %copy.129 = bf16[8,1,8192]{0,1,2:T(2,128)(2,1)} copy(bf16[8,1,8192]{2,0,1:T(8,128)(2,1)S(1)} %convert_element_type.228) | data formatting | bytes 262144 | tf_op jit(solution)/shard_map/convert_element_type | solution.py:134
  272.5 45.2 %reduce.1 = bf16[8192,8]{1,0:T(8,128)(2,1)S(1)} reduce(bf16[8192,1,8]{2,1,0:T(2,128)(2,1)} %bitcast.136, bf16[]{:T(256)} %broadcast.252), dimensions={1}, to_apply=%bitcast.114.reduce_sub_computation | reduce | bytes 262146
  320.7 11.2 %all-to-all-start.2 = ((bf16[64,2,512]{2,1,0:T(2,128)(2,1)}), bf16[64,2,512]{2,1,0:T(2,128)(2,1)S(1)}, u32[]{:S(2)}, u32[]{:S(2)}) async-start(bf16[64,2,512]{2,1,0:T(2,128)(2,1)} %reshape.221), calls=%async_computation.2 | async-start | bytes 262144 | tf_op jit(solution)/shard_map/all_to_all | solution.py:140
  331.9 8.7 %reshape.224 = bf16[8192,1,8]{2,1,0:T(2,128)(2,1)} reshape(bf16[64,2,512]{2,1,0:T(2,128)(2,1)S(1)} %all-to-all-done.4) | data formatting | bytes 262144
  340.6 7.8 %copy.145 = bf16[8,1,8192]{2,0,1:T(8,128)(2,1)S(1)} copy(bf16[8,1,8192]{0,1,2:T(2,128)(2,1)} %bitcast.138) | data formatting | bytes 262144 | tf_op jit(solution)/shard_map/all_to_all | solution.py:141
  348.5 8.7 %reshape.222 = bf16[8192,1,8]{2,1,0:T(2,128)(2,1)} reshape(bf16[64,2,512]{2,1,0:T(2,128)(2,1)S(1)} %all-to-all-done.2) | data formatting | bytes 262144
  357.3 7.8 %copy.130 = bf16[8,1,8192]{2,0,1:T(8,128)(2,1)S(1)} copy(bf16[8,1,8192]{0,1,2:T(2,128)(2,1)} %bitcast.139) | data formatting | bytes 262144 | tf_op jit(solution)/shard_map/all_to_all | solution.py:140
  (76 shorter events, 50.0 us)
Async XLA Ops:
  7.2 0.9 copy-start
  8.7 21.0 %all-to-all-start = ((bf16[1,64,128]{2,0,1:T(2,128)(2,1)}), bf16[1,64,128]{2,0,1:T(2,128)(2,1)S(1)}, u32[]{:S(2)}, u32[]{:S(2)}) async-start(bf16[1,64,128]{2,0,1:T(2,128)(2,1)} %copy.113), calls=%async_computation | async-start | bytes 65536 | tf_op jit(solution)/shard_map/all_to_all | solution.py:101
  29.8 47.1 %all-to-all-start.3 = ((bf16[8,64,128]{2,0,1:T(8,128)(2,1)}), bf16[8,64,128]{2,0,1:T(8,128)(2,1)S(1)}, u32[]{:S(2)}, u32[]{:S(2)}) async-start(bf16[8,64,128]{2,0,1:T(8,128)(2,1)} %copy.131), calls=%async_computation.3 | async-start | bytes 262144 | tf_op jit(solution)/shard_map/all_to_all | solution.py:94
  76.8 20.6 %all-to-all-start.1 = ((bf16[8,64,128]{2,0,1:T(8,128)(2,1)}), bf16[8,64,128]{2,0,1:T(8,128)(2,1)S(1)}, u32[]{:S(2)}, u32[]{:S(2)}) async-start(bf16[8,64,128]{2,0,1:T(8,128)(2,1)} %copy.114), calls=%async_computation.1 | async-start | bytes 262144 | tf_op jit(solution)/shard_map/all_to_all | solution.py:87
  99.7 4.9 %copy-start.1 = (f32[1024,128]{1,0:T(8,128)S(1)}, f32[1024,128]{1,0:T(8,128)}, u32[]{:S(2)}) copy-start(f32[1024,128]{1,0:T(8,128)} %all-gather.1) | copy-start | bytes 1572868
  99.7 4.9 %copy-start.2 = (f32[8,128,128]{2,1,0:T(8,128)S(1)}, f32[8,128,128]{2,1,0:T(8,128)}, u32[]{:S(2)}) copy-start(f32[8,128,128]{2,1,0:T(8,128)} %fusion.54) | copy-start | bytes 1572868
  168.3 65.7 %all-to-all-start.5 = ((f32[64,1,1024]{2,1,0:T(1,128)}), f32[64,1,1024]{2,1,0:T(1,128)}, u32[]{:S(2)}, u32[]{:S(2)}) async-start(f32[64,1,1024]{2,1,0:T(1,128)} %reshape.225), calls=%async_computation.5 | async-start | bytes 524288 | tf_op jit(solution)/shard_map/all_to_all | solution.py:151
  234.1 86.6 %all-to-all-start.4 = ((bf16[64,2,512]{2,1,0:T(2,128)(2,1)}), bf16[64,2,512]{2,1,0:T(2,128)(2,1)S(1)}, u32[]{:S(2)}, u32[]{:S(2)}) async-start(bf16[64,2,512]{2,1,0:T(2,128)(2,1)} %reshape.223), calls=%async_computation.4 | async-start | bytes 262144 | tf_op jit(solution)/shard_map/all_to_all | solution.py:141
  245.4 120.6 %reduce-scatter.2.cloned.1.call-start = ((), (), s32[]{:S(2)}) async-start(), calls=%async_computation.7 | async-start | bytes 294912 | tf_op jit(solution)/shard_map/reduce_scatter | solution.py:154
  320.7 27.8 %all-to-all-start.2 = ((bf16[64,2,512]{2,1,0:T(2,128)(2,1)}), bf16[64,2,512]{2,1,0:T(2,128)(2,1)S(1)}, u32[]{:S(2)}, u32[]{:S(2)}) async-start(bf16[64,2,512]{2,1,0:T(2,128)(2,1)} %reshape.221), calls=%async_computation.2 | async-start | bytes 262144 | tf_op jit(solution)/shard_map/all_to_all | solution.py:140
  348.5 16.6 %copy-start.3 = (bf16[512,128]{1,0:T(8,128)(2,1)S(1)}, bf16[512,128]{1,0:T(8,128)(2,1)}, u32[]{:S(2)}) copy-start(bf16[512,128]{1,0:T(8,128)(2,1)} %param.7) | copy-start | bytes 393220
  348.5 16.6 %copy-start.4 = (bf16[512,128]{1,0:T(8,128)(2,1)S(1)}, bf16[512,128]{1,0:T(8,128)(2,1)}, u32[]{:S(2)}) copy-start(bf16[512,128]{1,0:T(8,128)(2,1)} %param.6) | copy-start | bytes 393220
  348.5 16.6 %copy-start.5 = (bf16[512,128]{1,0:T(8,128)(2,1)S(1)}, bf16[512,128]{1,0:T(8,128)(2,1)}, u32[]{:S(2)}) copy-start(bf16[512,128]{1,0:T(8,128)(2,1)} %param.9) | copy-start | bytes 393220
Sparse Core Ops, SparseCore 0:
  265.0 39.2 reduce-scatter.1
where the time goes:
time: 382 us; the launch traced here: 375 us
  other arithmetic  136 us (36%)
  local copies, waits for them, and re-layouts  82.2 us (22%)
  starting transfers between devices  60.4 us (16%)
  blocking collectives  36.7 us (10%)
  matrix products  34.8 us (9%)
  between operations  15 us (4%)
  waiting for transfers between devices  9.6 us (3%)
    unnamed x3, other arithmetic  129 us
    unnamed x20, local copies, waits for them, and re-layouts  38.3 us
    dot_general x36, matrix products, contract(): jnp.einsum(form, left_side, right_side, precision=lax.Precision.HIGHEST)  34.8 us
    all_gather x1, blocking collectives, shards(): lax.all_gather(filt_real, 'ch', axis=0, tiled=True)  19.9 us
    all_gather x1, blocking collectives, shards(): lax.all_gather(filt_imag, 'ch', axis=0, tiled=True)  16.8 us
    all_to_all x1, starting transfers between devices, shards(): lax.all_to_all(filter_rows.reshape(-1, seq_count, tokens_dev), 'seq', spl...  12.4 us
    all_to_all x1, starting transfers between devices, shards(): lax.all_to_all(in_grad, 'seq', split_axis=2, concat_axis=1, tiled=True)  11.3 us
    all_to_all x1, starting transfers between devices, shards(): lax.all_to_all(conv_out, 'seq', split_axis=2, concat_axis=1, tiled=True)  11.2 us
  transfers between devices with their start and end apart: 7, of which 2 were waited for; matrix products, arithmetic and copies ran while one was open for 48% of the time, Pallas kernels for 0%

commit v1 on v0

v1 whole, which is shorter than its diff:
```python
import functools
import math

import jax
import jax.numpy as jnp
from jax import lax
from jax.experimental import pallas as pl
from jax.experimental.pallas import tpu as pltpu
from jax.sharding import PartitionSpec as P

TB = 128
BLK = 256
PARTS = 4
ORDER = (2, 1, 3, 0)
BF16 = jnp.bfloat16
F32 = jnp.float32


def dot(left, right, contract=((1,), (0,))):
    return lax.dot_general(left, right, (contract, ((), ())), preferred_element_type=F32)


def reversal(size):
    rows = lax.broadcasted_iota(jnp.int32, (size, size), 0)
    cols = lax.broadcasted_iota(jnp.int32, (size, size), 1)
    return (rows + cols == size - 1).astype(F32).astype(BF16)


def kernel(
    ns, nc,
    q_hbm, k_hbm, v_hbm, w_hbm, og_hbm,
    qg_out, kg_out, vg_out, fg_out,
    q_v, k_v, v_v, w_v, og_v,
    xa, ra, sd, mb, rb, fs, rf,
    ht, xf, xz0, xz8, gb, gjf, glt, lhs, acc, yst,
    xd, rd, mc, rc, fgm, fgs, rfg, rcf,
    in_sem, a_send, a_recv, b_send, b_recv, f_send, f_recv,
    d_send, d_recv, c_send, c_recv, g_send, g_recv,
):
    me_s, me_c = lax.axis_index("seq"), lax.axis_index("ch")
    pr = ns // PARTS
    nb = ns * TB // BLK
    rows = nb * nc
    msg = 2 * nc
    norm = float((ns * TB) ** -0.5)
    my_part = me_s // pr

    def copy_in(i, src, dst):
        return pltpu.make_async_copy(src, dst, in_sem.at[i])

    loads = [
        copy_in(0, k_hbm, k_v),
        copy_in(1, v_hbm, v_v),
        copy_in(2, og_hbm, og_v),
        copy_in(3, q_hbm, q_v),
        copy_in(4, w_hbm.at[pl.ds(pl.multiple_of(me_c * ns, ns), ns)], w_v),
    ]
    for load in loads:
        load.start()

    barrier = pltpu.get_barrier_semaphore()

    def greet_seq(o, carry):
        pl.semaphore_signal(barrier, inc=1, device_id={"seq": lax.rem(me_s + o, ns)})
        return carry

    def greet_ch(o, carry):
        pl.semaphore_signal(barrier, inc=1, device_id={"ch": lax.rem(me_c + o, nc)})
        return carry

    lax.fori_loop(1, nc, greet_ch, 0)
    lax.fori_loop(1, ns, greet_seq, 0)

    for load in loads:
        load.wait()

    def products(c, carry):
        for m in range(PARTS):
            at = pl.ds(pl.multiple_of(c * ns + m * pr, pr), pr)
            xa[m, c, 0] = (k_v[at].astype(F32) * v_v[at].astype(F32)).astype(BF16)
            xa[m, c, 1] = (og_v[at].astype(F32) * q_v[at].astype(F32)).astype(BF16)
        return carry

    lax.fori_loop(0, nc, products, 0)
    wf = w_v[...].astype(F32)
    for s in range(ns):
        fs[s] = wf[s : s + 1]

    pl.semaphore_wait(barrier, ns - 1 + nc - 1)

    def start_ch(out_ref, in_ref, send_sem, recv_sem):
        for kappa in ORDER:
            m = lax.rem(my_part + kappa, PARTS)

            def push(o, carry):
                c = lax.rem(me_c + o, nc)
                pltpu.make_async_remote_copy(
                    out_ref.at[m, c], in_ref.at[m, me_c], send_sem, recv_sem.at[kappa],
                    device_id={"ch": c},
                ).start()
                return carry

            lax.fori_loop(1, nc, push, 0)
            pltpu.make_async_copy(out_ref.at[m, me_c], in_ref.at[m, me_c], recv_sem.at[kappa]).start()

    def turn_part(kappa, in_ref, mid_ref, recv_sem):
        m = lax.rem(my_part + kappa, PARTS)
        pltpu.make_async_copy(in_ref.at[m], in_ref.at[m], recv_sem.at[kappa]).wait()
        sd[...] = in_ref[m].astype(F32).reshape(nc * 2 * pr, TB)
        for i in range(pr):
            upper = sd[pl.ds(i, nc, stride=2 * pr), :]
            lower = sd[pl.ds(pr + i, nc, stride=2 * pr), :]
            mid_ref[kappa, i] = jnp.concatenate([upper, lower], axis=0).astype(BF16)

    def start_seq_part(kappa, mid_ref, end_ref, send_sem, recv_sem):
        m = lax.rem(my_part + kappa, PARTS)
        mine = lax.rem(me_s, pr)

        def push(o, carry):
            i = lax.rem(mine + o, pr)
            pltpu.make_async_remote_copy(
                mid_ref.at[kappa, i], end_ref.at[me_s], send_sem, recv_sem,
                device_id={"seq": m * pr + i},
            ).start()
            return carry

        lax.fori_loop(1 if kappa == 0 else 0, pr, push, 0)
        if kappa == 0:
            pltpu.make_async_copy(mid_ref.at[kappa, mine], end_ref.at[me_s], recv_sem).start()

    def start_rows(out_ref, in_ref, send_sem, recv_sem):
        def push(o, carry):
            s = lax.rem(me_s + o, ns)
            pltpu.make_async_remote_copy(
                out_ref.at[s], in_ref.at[me_s], send_sem, recv_sem, device_id={"seq": s}
            ).start()
            return carry

        lax.fori_loop(1, ns, push, 0)
        pltpu.make_async_copy(out_ref.at[me_s], in_ref.at[me_s], recv_sem).start()

    def wait_all(ref, sem):
        pltpu.make_async_copy(ref, ref, sem).wait()

    start_ch(xa, ra, a_send, a_recv)
    start_rows(fs, rf, f_send, f_recv)
    for kappa in ORDER:
        turn_part(kappa, ra, mb, a_recv)
        start_seq_part(kappa, mb, rb, b_send, b_recv)

    wait_all(rf, f_recv)
    sub = lax.broadcasted_iota(jnp.int32, (TB, TB), 0)
    lane = lax.broadcasted_iota(jnp.int32, (TB, TB), 1)
    keep = lane >= sub
    ht[:, 0:TB] = jnp.zeros((TB, TB), BF16)

    def toeplitz(e, before):
        turned = pltpu.roll(jnp.broadcast_to(rf[e], (TB, TB)), 0, 1, stride=1, stride_axis=0)
        at = pl.ds(pl.multiple_of((e + 1) * TB, TB), TB)
        ht[:, at] = jnp.where(keep, turned, before).astype(BF16)
        return turned

    lax.fori_loop(0, ns, toeplitz, jnp.zeros((TB, TB), F32))
    acc[...] = jnp.zeros_like(acc)
    xf[0:rows] = jnp.zeros((rows, BLK), F32)
    xf[2 * rows :] = jnp.zeros((nc, BLK), F32)
    flip = reversal(BLK)

    wait_all(rb, b_recv)

    def gather(j, carry):
        low, high = rb[2 * j].astype(F32), rb[2 * j + 1].astype(F32)
        at = pl.ds(pl.multiple_of(rows + j * nc, nc), nc)
        xf[at, 0:TB] = low[0:nc]
        xf[at, TB:BLK] = high[0:nc]
        at = pl.ds(pl.multiple_of(j * nc, nc), nc)
        gjf[at, 0:TB] = low[nc:msg]
        gjf[at, TB:BLK] = high[nc:msg]
        return carry

    lax.fori_loop(0, nb, gather, 0)
    gb[...] = gjf[...].astype(BF16)
    gjf[...] = dot(gb[...], flip)

    def interleave(j, carry):
        x_at = pl.ds(pl.multiple_of(rows + j * nc, nc), nc)
        g_at = pl.ds(pl.multiple_of((nb - 1 - j) * nc, nc), nc)
        both = jnp.concatenate([xf[x_at], gjf[g_at]], axis=0)
        lhs[pl.ds(pl.multiple_of(j * msg, msg), msg)] = both.astype(BF16)
        return carry

    lax.fori_loop(0, nb, interleave, 0)

    group = nb // PARTS
    for grp in range(PARTS):
        count = (nb - grp * group) * msg

        def lag(i, carry):
            d = grp * group + i
            low = pl.multiple_of(d * BLK, BLK)
            block = jnp.concatenate([ht[:, pl.ds(low + TB, BLK)], ht[:, pl.ds(low, BLK)]], axis=0)
            at = pl.ds(pl.multiple_of(d * msg, msg), count)
            acc[at] += dot(lhs[0:count], block)
            return carry

        lax.fori_loop(0, group, lag, 0)

    def scatter_x(j, carry):
        out = acc[pl.ds(pl.multiple_of(j * msg, msg), nc)] * norm
        yst[pl.ds(pl.multiple_of(2 * j * msg, msg), nc)] = out[:, 0:TB]
        yst[pl.ds(pl.multiple_of((2 * j + 1) * msg, msg), nc)] = out[:, TB:BLK]
        gjf[pl.ds(pl.multiple_of((nb - 1 - j) * nc, nc), nc)] = (
            acc[pl.ds(pl.multiple_of(j * msg + nc, nc), nc)] * norm
        )
        return carry

    lax.fori_loop(0, nb, scatter_x, 0)
    gjf[...] = dot(gjf[...].astype(BF16), flip)

    def scatter_g(j, carry):
        out = gjf[pl.ds(pl.multiple_of(j * nc, nc), nc)]
        yst[pl.ds(pl.multiple_of(2 * j * msg + nc, nc), nc)] = out[:, 0:TB]
        yst[pl.ds(pl.multiple_of((2 * j + 1) * msg + nc, nc), nc)] = out[:, TB:BLK]
        return carry

    lax.fori_loop(0, nb, scatter_g, 0)

    for m in range(PARTS):
        for c in range(nc):
            for part in range(2):
                first = m * pr * msg + part * nc + c
                xd[m, c, part] = yst[pl.ds(first, pr, stride=msg), :].astype(BF16)
    start_ch(xd, rd, d_send, d_recv)

    glt[...] = dot(flip, gb[...], ((1,), (1,))).astype(BF16)
    xz0[...] = xf[0 : 2 * rows].astype(BF16)
    xz8[...] = xf[nc : 2 * rows + nc].astype(BF16)

    def diagonals(tile, before, at):
        turned = pltpu.roll(tile, 0, 1, stride=1, stride_axis=0)
        fgm[pl.ds(at, 1)] = jnp.sum(jnp.where(keep, turned, before), axis=0, keepdims=True)
        return turned

    def two_lags(i, carry):
        over, before = carry
        odd = pl.multiple_of((2 * i) * nc, msg)
        even = pl.multiple_of((2 * i + 2) * nc, msg)
        for half, shifted in ((0, xz8[pl.ds(odd, rows)]), (1, xz0[pl.ds(even, rows)])):
            prod = dot(glt[...], shifted)
            at = 4 * i + 2 * half
            before = diagonals(prod[0:TB, 0:TB] + over, before, at)
            before = diagonals(prod[0:TB, TB:BLK] + prod[TB:BLK, 0:TB], before, at + 1)
            over = prod[TB:BLK, TB:BLK]
        return over, before

    zero = jnp.zeros((TB, TB), F32)
    lax.fori_loop(0, nb // 2, two_lags, (zero, zero))

    for kappa in ORDER:
        turn_part(kappa, rd, mc, d_recv)
        start_seq_part(kappa, mc, rc, c_send, c_recv)

    fgm[...] = dot((fgm[...] * norm).astype(BF16), reversal(TB))
    for s in range(ns):
        fgs[s] = fgm[ns - 1 - s : ns - s]
    start_rows(fgs, rfg, g_send, g_recv)

    wait_all(rc, c_recv)
    rcf[...] = rc[...].astype(F32).reshape(ns * msg, TB)
    for c in range(nc):
        at = pl.ds(c * ns, ns)
        conv = rcf[pl.ds(c, ns, stride=msg), :]
        grad = rcf[pl.ds(nc + c, ns, stride=msg), :]
        qg_out[at] = (og_v[at].astype(F32) * conv).astype(BF16)
        kg_out[at] = (grad * v_v[at].astype(F32)).astype(BF16)
        vg_out[at] = (grad * k_v[at].astype(F32)).astype(BF16)

    wait_all(rfg, g_recv)
    for s in range(ns):
        fgm[s : s + 1] = rfg[s]
    fg_out[...] = fgm[...].astype(BF16)

    wait_all(xa.at[:, pl.ds(0, nc - 1)], a_send)
    wait_all(xd.at[:, pl.ds(0, nc - 1)], d_send)
    for ref, sem in ((rb, b_send), (rc, c_send), (fs, f_send), (fgs, g_send)):
        wait_all(ref.at[pl.ds(0, ns - 1)], sem)


def shards(ns, nc, query_gate, key_gate, value_in, filter_weight, output_grad):
    local = query_gate.shape[0]
    nb = ns * TB // BLK
    rows, msg, pr = nb * nc, 2 * nc, ns // PARTS
    bf, f32 = (lambda *shape: pltpu.VMEM(shape, BF16)), (lambda *shape: pltpu.VMEM(shape, F32))
    one = pltpu.SemaphoreType.DMA(())
    some = pltpu.SemaphoreType.DMA((PARTS,))
    any_spec = pl.BlockSpec(memory_space=pl.ANY)
    vmem_spec = pl.BlockSpec(memory_space=pltpu.VMEM)
    wide = jax.ShapeDtypeStruct((local, TB), BF16)
    return pl.pallas_call(
        functools.partial(kernel, ns, nc),
        out_shape=(wide, wide, wide, jax.ShapeDtypeStruct((ns, TB), BF16)),
        in_specs=[any_spec] * 5,
        out_specs=(vmem_spec,) * 4,
        scratch_shapes=[
            bf(local, TB), bf(local, TB), bf(local, TB), bf(ns, TB), bf(local, TB),
            bf(PARTS, nc, 2, pr, TB), bf(PARTS, nc, 2, pr, TB), f32(nc * 2 * pr, TB),
            bf(PARTS, pr, msg, TB), bf(ns, msg, TB), f32(ns, 1, TB), f32(ns, 1, TB),
            bf(TB, (ns + 1) * TB), f32(2 * rows + nc, BLK), bf(2 * rows, BLK), bf(2 * rows, BLK),
            bf(rows, BLK), f32(rows, BLK), bf(BLK, rows), bf(2 * rows, BLK),
            f32(2 * rows + 2 * rows // PARTS, BLK), f32(ns * msg, TB),
            bf(PARTS, nc, 2, pr, TB), bf(PARTS, nc, 2, pr, TB),
            bf(PARTS, pr, msg, TB), bf(ns, msg, TB), f32(ns, TB), f32(ns, 1, TB), f32(ns, 1, TB),
            f32(ns * msg, TB),
            pltpu.SemaphoreType.DMA((5,)), one, some, one, one, one, one,
            one, some, one, one, one, one,
        ],
        compiler_params=pltpu.CompilerParams(
            collective_id=0, has_side_effects=True, vmem_limit_bytes=40 * 1024 * 1024
        ),
    )(query_gate, key_gate, value_in, filter_weight, output_grad)


def solution(mesh):
    ns, nc = mesh.shape["seq"], mesh.shape["ch"]
    placed = (P("ch", "seq"), P("ch", "seq"), P("ch", "seq"), P(None, "seq"), P("ch", "seq"))
    return jax.shard_map(
        functools.partial(shards, ns, nc),
        mesh=mesh,
        in_specs=placed,
        out_specs=(P("ch", "seq"),) * 4,
        check_vma=False,
    )
```

time: 382 us -> 67 us (0.18)
  the two profiles are of different devices: /device:TPU:6 before, /device:TPU:1 now
where the time goes in v1:
time: 67 us; the launch traced here: 66.8 us
  Pallas kernels  59 us (88%)
  local copies, waits for them, and re-layouts  7.08 us (11%)
    pallas_call x1, Pallas kernels, shards(): pl.pallas_call(functools.partial(kernel, ns, nc), out_shape=(wide, wide,...  59 us
    unnamed x14, local copies, waits for them, and re-layouts  7.08 us

profile of v1, /device:TPU:1, one launch (start us, length us, event | category | flops | bytes accessed | tf_op | source)
XLA Modules:
  0.0 66.8 jit_solution(1993729564918897559)
XLA Ops:
  0.6 0.0 copy-start
  0.6 0.9 %copy-done = bf16[512,128]{1,0:T(8,128)(2,1)S(1)} copy-done((bf16[512,128]{1,0:T(8,128)(2,1)S(1)}, bf16[512,128]{1,0:T(8,128)(2,1)}, u32[]{:S(2)}) %copy-start) | copy-done | bytes 131096
  1.5 0.0 copy-start.1
  1.5 0.9 %copy-done.1 = bf16[512,128]{1,0:T(8,128)(2,1)S(1)} copy-done((bf16[512,128]{1,0:T(8,128)(2,1)S(1)}, bf16[512,128]{1,0:T(8,128)(2,1)}, u32[]{:S(2)}) %copy-start.1) | copy-done | bytes 131096
  2.4 0.0 copy-start.2
  2.4 0.9 %copy-done.2 = bf16[512,128]{1,0:T(8,128)(2,1)S(1)} copy-done((bf16[512,128]{1,0:T(8,128)(2,1)S(1)}, bf16[512,128]{1,0:T(8,128)(2,1)}, u32[]{:S(2)}) %copy-start.2) | copy-done | bytes 131096
  3.3 0.0 copy-start.3
  3.3 0.9 %copy-done.3 = bf16[512,128]{1,0:T(8,128)(2,1)S(1)} copy-done((bf16[512,128]{1,0:T(8,128)(2,1)S(1)}, bf16[512,128]{1,0:T(8,128)(2,1)}, u32[]{:S(2)}) %copy-start.3) | copy-done | bytes 131096
  4.3 0.0 copy-start.4
  4.3 0.9 %copy-done.4 = bf16[512,128]{1,0:T(8,128)(2,1)S(1)} copy-done((bf16[512,128]{1,0:T(8,128)(2,1)S(1)}, bf16[512,128]{1,0:T(8,128)(2,1)}, u32[]{:S(2)}) %copy-start.4) | copy-done | bytes 131096
  5.2 59.0 %shard_map.84 = (bf16[512,128]{1,0:T(8,128)(2,1)S(1)}, bf16[512,128]{1,0:T(8,128)(2,1)S(1)}, bf16[512,128]{1,0:T(8,128)(2,1)S(1)}, bf16[64,128]{1,0:T(8,128)(2,1)S(1)}) custom-call(bf16[512,128]{1,0:T(8,128)(2,1)S(1)} %copy-done, bf16[512,128]{1,0:T(8,128)(2,1)S(1)} %copy-done.1, bf16[512,128]{1,0:T(8,128)(2,1)S(1)} %copy-done.2, ...), custom_call_target="tpu_custom_call" | custom-call | tf_op jit(solution)/shard_map/pallas_call | solution.py:299
  64.2 0.7 copy.13
  64.9 0.7 copy.14
  65.5 0.7 copy.15
  66.2 0.6 copy.16
Async XLA Ops:
  0.6 0.9 %copy-start = (bf16[512,128]{1,0:T(8,128)(2,1)S(1)}, bf16[512,128]{1,0:T(8,128)(2,1)}, u32[]{:S(2)}) copy-start(bf16[512,128]{1,0:T(8,128)(2,1)} %q_hbm.1) | copy-start | bytes 393220
  1.5 0.9 %copy-start.1 = (bf16[512,128]{1,0:T(8,128)(2,1)S(1)}, bf16[512,128]{1,0:T(8,128)(2,1)}, u32[]{:S(2)}) copy-start(bf16[512,128]{1,0:T(8,128)(2,1)} %k_hbm.1) | copy-start | bytes 393220
  2.4 0.9 %copy-start.2 = (bf16[512,128]{1,0:T(8,128)(2,1)S(1)}, bf16[512,128]{1,0:T(8,128)(2,1)}, u32[]{:S(2)}) copy-start(bf16[512,128]{1,0:T(8,128)(2,1)} %v_hbm.1) | copy-start | bytes 393220
  3.3 0.9 %copy-start.3 = (bf16[512,128]{1,0:T(8,128)(2,1)S(1)}, bf16[512,128]{1,0:T(8,128)(2,1)}, u32[]{:S(2)}) copy-start(bf16[512,128]{1,0:T(8,128)(2,1)} %w_hbm.1) | copy-start | bytes 393220
  4.3 0.9 %copy-start.4 = (bf16[512,128]{1,0:T(8,128)(2,1)S(1)}, bf16[512,128]{1,0:T(8,128)(2,1)}, u32[]{:S(2)}) copy-start(bf16[512,128]{1,0:T(8,128)(2,1)} %og_hbm.1) | copy-start | bytes 393220

commit v2 on v1

v2 whole, which is shorter than its diff:
```python
import functools
import math

import jax
import jax.numpy as jnp
from jax import lax
from jax.experimental import pallas as pl
from jax.experimental.pallas import tpu as pltpu
from jax.sharding import PartitionSpec as P

TB = 128
BLK = 256
PARTS = 4
ORDER = (2, 1, 3, 0)
LAGS = 4
VMEM_BYTES = 60 * 1024 * 1024
BF16 = jnp.bfloat16
F32 = jnp.float32


def dot(left, right, contract=((1,), (0,))):
    return lax.dot_general(left, right, (contract, ((), ())), preferred_element_type=F32)


def reversal(size):
    rows = lax.broadcasted_iota(jnp.int32, (size, size), 0)
    cols = lax.broadcasted_iota(jnp.int32, (size, size), 1)
    return (rows + cols == size - 1).astype(F32).astype(BF16)


def kernel(
    ns, nc, nu,
    q_hbm, k_hbm, v_hbm, w_hbm, og_hbm,
    rc, g2,
    q_v, k_v, v_v, w_v, og_v,
    xa, ra, sd, mb, rb, fs, f1, f1s, f2,
    tt, xf, xz0, xz8, gb, gjf, glt, lhs, acc, yst,
    xd, rd, mc, fgm, g1, g1s,
    in_sem, a_send, a_recv, b_send, b_recv, f_send, f_recv,
    d_send, d_recv, c_send, c_recv, g_send, g_recv,
):
    me_s, me_c = lax.axis_index("seq"), lax.axis_index("ch")
    ny = ns // nu
    me_y, me_u = me_s // nu, lax.rem(me_s, nu)
    pr = ns // PARTS
    nb = ns * TB // BLK
    rows = nb * nc
    msg = 2 * nc
    norm = float((ns * TB) ** -0.5)
    my_part = me_s // pr

    def copy_in(i, src, dst):
        return pltpu.make_async_copy(src, dst, in_sem.at[i])

    loads = [
        copy_in(0, k_hbm, k_v),
        copy_in(1, v_hbm, v_v),
        copy_in(2, og_hbm, og_v),
        copy_in(3, q_hbm, q_v),
        copy_in(4, w_hbm.at[pl.ds(pl.multiple_of(me_c * ns, ns), ns)], w_v),
    ]
    for load in loads:
        load.start()

    barrier = pltpu.get_barrier_semaphore()

    def greet_seq(o, carry):
        pl.semaphore_signal(barrier, inc=1, device_id={"seq": lax.rem(me_s + o, ns)})
        return carry

    def greet_ch(o, carry):
        pl.semaphore_signal(barrier, inc=1, device_id={"ch": lax.rem(me_c + o, nc)})
        return carry

    lax.fori_loop(1, nc, greet_ch, 0)
    lax.fori_loop(1, ns, greet_seq, 0)

    for load in loads:
        load.wait()

    for c in range(nc):
        for m in range(PARTS):
            at = pl.ds(c * ns + m * pr, pr)
            xa[m, c, 0] = (k_v[at].astype(F32) * v_v[at].astype(F32)).astype(BF16)
            xa[m, c, 1] = (og_v[at].astype(F32) * q_v[at].astype(F32)).astype(BF16)
    fs[...] = w_v[...].astype(F32)

    pl.semaphore_wait(barrier, ns - 1 + nc - 1)

    def tile(ref, i, size):
        return ref.at[pl.ds(pl.multiple_of(i * size, size), size)]

    def start_y(out_ref, in_ref, send_sem, recv_sem):
        def push(o, carry):
            y = lax.rem(me_y + o, ny)
            pltpu.make_async_remote_copy(
                tile(out_ref, y, nu), tile(in_ref, me_y, nu), send_sem.at[0], recv_sem.at[0],
                device_id={"seq": y * nu + me_u},
            ).start()
            return carry

        lax.fori_loop(1, ny, push, 0)
        pltpu.make_async_copy(
            tile(out_ref, me_y, nu), tile(in_ref, me_y, nu), recv_sem.at[0]
        ).start()

    def turn_y_start_u(in_ref, mid_ref, end_ref, send_sem, recv_sem):
        wait_all(in_ref, recv_sem.at[0])
        for u in range(nu):
            mid_ref[u * ny : (u + 1) * ny] = in_ref[pl.ds(u, ny, stride=nu), :]

        def push(o, carry):
            u = lax.rem(me_u + o, nu)
            pltpu.make_async_remote_copy(
                tile(mid_ref, u, ny), tile(end_ref, me_u, ny), send_sem.at[1], recv_sem.at[1],
                device_id={"seq": me_y * nu + u},
            ).start()
            return carry

        lax.fori_loop(1, nu, push, 0)
        pltpu.make_async_copy(
            tile(mid_ref, me_u, ny), tile(end_ref, me_u, ny), recv_sem.at[1]
        ).start()

    def start_ch(out_ref, in_ref, send_sem, recv_sem):
        for kappa in ORDER:
            m = lax.rem(my_part + kappa, PARTS)

            def push(o, carry):
                c = lax.rem(me_c + o, nc)
                pltpu.make_async_remote_copy(
                    out_ref.at[m, c], in_ref.at[m, me_c], send_sem, recv_sem.at[kappa],
                    device_id={"ch": c},
                ).start()
                return carry

            lax.fori_loop(1, nc, push, 0)
            pltpu.make_async_copy(out_ref.at[m, me_c], in_ref.at[m, me_c], recv_sem.at[kappa]).start()

    def turn_part(kappa, in_ref, mid_ref, recv_sem):
        m = lax.rem(my_part + kappa, PARTS)
        wait_all(in_ref.at[m], recv_sem.at[kappa])
        sd[...] = in_ref[m].astype(F32).reshape(nc * 2 * pr, TB)
        for i in range(pr):
            upper = sd[pl.ds(i, nc, stride=2 * pr), :]
            lower = sd[pl.ds(pr + i, nc, stride=2 * pr), :]
            mid_ref[kappa, i] = jnp.concatenate([upper, lower], axis=0).astype(BF16)

    def start_seq_part(kappa, mid_ref, end_ref, send_sem, recv_sem):
        m = lax.rem(my_part + kappa, PARTS)
        mine = lax.rem(me_s, pr)

        def push(o, carry):
            i = lax.rem(mine + o, pr)
            pltpu.make_async_remote_copy(
                mid_ref.at[kappa, i], end_ref.at[me_s], send_sem, recv_sem,
                device_id={"seq": m * pr + i},
            ).start()
            return carry

        lax.fori_loop(1 if kappa == 0 else 0, pr, push, 0)
        if kappa == 0:
            pltpu.make_async_copy(mid_ref.at[kappa, mine], end_ref.at[me_s], recv_sem).start()

    def wait_all(ref, sem):
        pltpu.make_async_copy(ref, ref, sem).wait()

    start_y(fs, f1, f_send, f_recv)
    start_ch(xa, ra, a_send, a_recv)
    turn_y_start_u(f1, f1s, f2, f_send, f_recv)
    for kappa in ORDER:
        turn_part(kappa, ra, mb, a_recv)
        start_seq_part(kappa, mb, rb, b_send, b_recv)

    sub = lax.broadcasted_iota(jnp.int32, (TB, TB), 0)
    lane = lax.broadcasted_iota(jnp.int32, (TB, TB), 1)
    keep = lane >= sub
    zero = jnp.zeros((TB, TB), F32)
    flip = reversal(BLK)
    wait_all(f2, f_recv.at[1])

    def skewed(tile):
        return pltpu.roll(tile, 0, 1, stride=1, stride_axis=0)

    def filter_row(s):
        return jnp.broadcast_to(f2[pl.ds(s % nu * ny + s // nu, 1), :], (TB, TB))

    tt[TB:BLK, 0:TB] = zero.astype(BF16)
    before = zero
    for d in range(nb):
        even, odd = skewed(filter_row(2 * d)), skewed(filter_row(2 * d + 1))
        block = jnp.where(keep, even, before).astype(BF16)
        tt[d * BLK : d * BLK + TB, 0:TB] = block
        tt[d * BLK + TB : (d + 1) * BLK, TB:BLK] = block
        block = jnp.where(keep, odd, even).astype(BF16)
        tt[d * BLK : d * BLK + TB, TB:BLK] = block
        tt[(d + 1) * BLK + TB : (d + 2) * BLK, 0:TB] = block
        before = odd

    lhs[0 : LAGS * msg] = jnp.zeros((LAGS * msg, BLK), BF16)
    xf[0:rows] = jnp.zeros((rows, BLK), F32)
    xf[2 * rows :] = jnp.zeros((nc, BLK), F32)

    wait_all(rb, b_recv)
    for j in range(nb):
        low, high = rb[2 * j].astype(F32), rb[2 * j + 1].astype(F32)
        xf[rows + j * nc : rows + (j + 1) * nc, 0:TB] = low[0:nc]
        xf[rows + j * nc : rows + (j + 1) * nc, TB:BLK] = high[0:nc]
        gjf[j * nc : (j + 1) * nc, 0:TB] = low[nc:msg]
        gjf[j * nc : (j + 1) * nc, TB:BLK] = high[nc:msg]
    gb[...] = gjf[...].astype(BF16)
    gjf[...] = dot(gb[...], flip)
    for j in range(nb):
        back = nb - 1 - j
        both = jnp.concatenate(
            [xf[rows + j * nc : rows + (j + 1) * nc], gjf[back * nc : (back + 1) * nc]], axis=0
        )
        lhs[(LAGS + j) * msg : (LAGS + j + 1) * msg] = both.astype(BF16)

    for first in range(0, nb, LAGS):
        count = (nb - first) * msg
        left = jnp.concatenate(
            [lhs[(LAGS - e) * msg : (LAGS - e) * msg + count] for e in range(LAGS)], axis=1
        )
        prod = dot(left, tt[first * BLK : (first + LAGS) * BLK])
        if first == 0:
            acc[...] = prod
        else:
            acc[first * msg :] += prod

    for j in range(nb):
        back = nb - 1 - j
        out = acc[j * msg : j * msg + nc] * norm
        yst[2 * j * msg : 2 * j * msg + nc] = out[:, 0:TB]
        yst[(2 * j + 1) * msg : (2 * j + 1) * msg + nc] = out[:, TB:BLK]
        gjf[back * nc : (back + 1) * nc] = acc[j * msg + nc : (j + 1) * msg] * norm
    gjf[...] = dot(gjf[...].astype(BF16), flip)
    for j in range(nb):
        out = gjf[j * nc : (j + 1) * nc]
        yst[2 * j * msg + nc : (2 * j + 1) * msg] = out[:, 0:TB]
        yst[(2 * j + 1) * msg + nc : (2 * j + 2) * msg] = out[:, TB:BLK]

    for m in range(PARTS):
        for c in range(nc):
            for part in range(2):
                begin = m * pr * msg + part * nc + c
                xd[m, c, part] = yst[pl.ds(begin, pr, stride=msg), :].astype(BF16)
    start_ch(xd, rd, d_send, d_recv)

    glt[...] = dot(flip, gb[...], ((1,), (1,))).astype(BF16)
    xz0[...] = xf[0 : 2 * rows].astype(BF16)
    xz8[...] = xf[nc : 2 * rows + nc].astype(BF16)
    over, before = zero, zero
    for i in range(nb):
        low = (i // 2) * msg
        shifted = xz0[low + msg : low + msg + rows] if i % 2 else xz8[low : low + rows]
        prod = dot(glt[...], shifted)
        pair = (prod[0:TB, 0:TB] + over, prod[0:TB, TB:BLK] + prod[TB:BLK, 0:TB])
        for half, total in enumerate(pair):
            at = ns - 1 - (2 * i + half)
            turned = skewed(total)
            fgm[at : at + 1] = jnp.sum(jnp.where(keep, turned, before), axis=0, keepdims=True)
            before = turned
        over = prod[TB:BLK, TB:BLK]
    fgm[...] = dot((fgm[...] * norm).astype(BF16), reversal(TB))
    start_y(fgm, g1, g_send, g_recv)

    for kappa in ORDER:
        turn_part(kappa, rd, mc, d_recv)
        start_seq_part(kappa, mc, rc, c_send, c_recv)
    turn_y_start_u(g1, g1s, g2, g_send, g_recv)

    wait_all(rc, c_recv)
    wait_all(g2, g_recv.at[1])
    wait_all(xa.at[:, pl.ds(0, nc - 1)], a_send)
    wait_all(xd.at[:, pl.ds(0, nc - 1)], d_send)
    for ref, sem in ((rb, b_send), (rc, c_send)):
        wait_all(ref.at[pl.ds(0, ns - 1)], sem)
    for sem in (f_send, g_send):
        wait_all(f1.at[pl.ds(0, ns - nu)], sem.at[0])
        wait_all(f2.at[pl.ds(0, ns - ny)], sem.at[1])


def finish(ns, nc, nu, rc, g2, k_v, v_v, og_v, qg_out, kg_out, vg_out, fg_out, rcf):
    msg, ny = 2 * nc, ns // nu
    rcf[...] = rc[...].astype(F32).reshape(ns * msg, TB)
    for c in range(nc):
        at = pl.ds(c * ns, ns)
        conv = rcf[pl.ds(c, ns, stride=msg), :]
        grad = rcf[pl.ds(nc + c, ns, stride=msg), :]
        qg_out[at] = (og_v[at].astype(F32) * conv).astype(BF16)
        kg_out[at] = (grad * v_v[at].astype(F32)).astype(BF16)
        vg_out[at] = (grad * k_v[at].astype(F32)).astype(BF16)
    for y in range(0, ny, 2):
        two = [g2[pl.ds(y + i, nu, stride=ny), :] for i in range(2)]
        fg_out[y * nu : (y + 2) * nu] = jnp.concatenate(two, axis=0).astype(BF16)


def shards(ns, nc, query_gate, key_gate, value_in, filter_weight, output_grad):
    local = query_gate.shape[0]
    nb, nu = ns * TB // BLK, math.isqrt(ns)
    ny = ns // nu
    rows, msg, pr = nb * nc, 2 * nc, ns // PARTS
    bf, f32 = (lambda *shape: pltpu.VMEM(shape, BF16)), (lambda *shape: pltpu.VMEM(shape, F32))
    one = pltpu.SemaphoreType.DMA(())
    two = pltpu.SemaphoreType.DMA((2,))
    some = pltpu.SemaphoreType.DMA((PARTS,))
    any_spec = pl.BlockSpec(memory_space=pl.ANY)
    vmem_spec = pl.BlockSpec(memory_space=pltpu.VMEM)
    moved, filter_part = pl.pallas_call(
        functools.partial(kernel, ns, nc, nu),
        out_shape=(
            jax.ShapeDtypeStruct((ns, msg, TB), BF16),
            jax.ShapeDtypeStruct((ns, TB), F32),
        ),
        in_specs=[any_spec] * 5,
        out_specs=(any_spec,) * 2,
        scratch_shapes=[
            bf(local, TB), bf(local, TB), bf(local, TB), bf(ns, TB), bf(local, TB),
            bf(PARTS, nc, 2, pr, TB), bf(PARTS, nc, 2, pr, TB), f32(nc * 2 * pr, TB),
            bf(PARTS, pr, msg, TB), bf(ns, msg, TB),
            f32(ns, TB), f32(ns, TB), f32(ns, TB), f32(ns, TB),
            bf((nb + 1) * BLK, BLK), f32(2 * rows + nc, BLK), bf(2 * rows, BLK), bf(2 * rows, BLK),
            bf(rows, BLK), f32(rows, BLK), bf(BLK, rows), bf((LAGS + nb) * msg, BLK),
            f32(nb * msg, BLK), f32(ns * msg, TB),
            bf(PARTS, nc, 2, pr, TB), bf(PARTS, nc, 2, pr, TB),
            bf(PARTS, pr, msg, TB), f32(ns, TB), f32(ns, TB), f32(ns, TB),
            pltpu.SemaphoreType.DMA((5,)), one, some, one, one, two, two,
            one, some, one, one, two, two,
        ],
        compiler_params=pltpu.CompilerParams(
            collective_id=0, has_side_effects=True, vmem_limit_bytes=VMEM_BYTES
        ),
    )(query_gate, key_gate, value_in, filter_weight, output_grad)
    wide = jax.ShapeDtypeStruct((local, TB), BF16)
    return pl.pallas_call(
        functools.partial(finish, ns, nc, nu),
        out_shape=(wide, wide, wide, jax.ShapeDtypeStruct((ns, TB), BF16)),
        in_specs=[vmem_spec] * 5,
        out_specs=(vmem_spec,) * 4,
        scratch_shapes=[f32(ns * msg, TB)],
        compiler_params=pltpu.CompilerParams(vmem_limit_bytes=VMEM_BYTES),
    )(moved, filter_part, key_gate, value_in, output_grad)


def solution(mesh):
    ns, nc = mesh.shape["seq"], mesh.shape["ch"]
    placed = (P("ch", "seq"), P("ch", "seq"), P("ch", "seq"), P(None, "seq"), P("ch", "seq"))
    return jax.shard_map(
        functools.partial(shards, ns, nc),
        mesh=mesh,
        in_specs=placed,
        out_specs=(P("ch", "seq"),) * 4,
        check_vma=False,
    )
```

time: 67 us -> 54.5 us (0.81)
  local copies, waits for them, and re-layouts: 7.08 us -> 0 us
  Pallas kernels: 59 us -> 53.7 us
    unnamed x14 -> x0, local copies, waits for them, and re-layouts: 7.08 us -> none
    pallas_call x1 -> x2, Pallas kernels: 59 us -> 53.7 us  [the longest x1 51.6 us: shards(): pl.pallas_call(functools.partial(kernel, ns, nc, nu), out_shape=(jax.Shap...]
where the time goes in v2:
time: 54.5 us; the launch traced here: 54.3 us
  Pallas kernels  53.7 us (99%)
  between operations  0.64 us (1%)
    pallas_call x1, Pallas kernels, shards(): pl.pallas_call(functools.partial(kernel, ns, nc, nu), out_shape=(jax.Shap...  51.6 us
    pallas_call x1, Pallas kernels, shards(): pl.pallas_call(functools.partial(finish, ns, nc, nu), out_shape=(wide, wi...  2.09 us

profile of v2, /device:TPU:1, one launch (start us, length us, event | category | flops | bytes accessed | tf_op | source)
XLA Modules:
  0.0 54.3 jit_solution(89969413716358487)
XLA Ops:
  0.6 51.6 %shard_map.84 = (bf16[64,16,128]{2,1,0:T(8,128)(2,1)}, f32[64,128]{1,0:T(8,128)}) custom-call(bf16[512,128]{1,0:T(8,128)(2,1)} %q_hbm.1, bf16[512,128]{1,0:T(8,128)(2,1)} %k_v.1, bf16[512,128]{1,0:T(8,128)(2,1)} %v_v.1, bf16[512,128]{1,0:T(8,128)(2,1)} %w_hbm.1, bf16[512,128]{1,0:T(8,128)(2,1)} %og_v.1), custom_call_target="tpu_custom_call" | custom-call | tf_op jit(solution)/shard_map/pallas_call | solution.py:310
  52.3 2.1 %shard_map.85 = (bf16[512,128]{1,0:T(8,128)(2,1)}, bf16[512,128]{1,0:T(8,128)(2,1)}, bf16[512,128]{1,0:T(8,128)(2,1)}, bf16[64,128]{1,0:T(8,128)(2,1)}) custom-call(bf16[64,16,128]{2,1,0:T(8,128)(2,1)} %get-tuple-element.6.rc, f32[64,128]{1,0:T(8,128)} %get-tuple-element.7.g2, bf16[512,128]{1,0:T(8,128)(2,1)} %k_v.1, bf16[512,128]{1,0:T(8,128)(2,1)} %v_v.1, ...), custom_call_target="tpu_custom_call" | custom-call | tf_op jit(solution)/shard_map/pallas_call | solution.py:336

commit v3 on v2

v3 whole, which is shorter than its diff:
```python
import functools
import math

import jax
import jax.numpy as jnp
from jax import lax
from jax.experimental import pallas as pl
from jax.experimental.pallas import tpu as pltpu
from jax.sharding import PartitionSpec as P

TB = 128
BLK = 256
PARTS = 4
ORDER = (2, 1, 3, 0)
LAGS = 4
VMEM_BYTES = 60 * 1024 * 1024
BF16 = jnp.bfloat16
F32 = jnp.float32


def dot(left, right, contract=((1,), (0,))):
    return lax.dot_general(left, right, (contract, ((), ())), preferred_element_type=F32)


def reversal(size):
    rows = lax.broadcasted_iota(jnp.int32, (size, size), 0)
    cols = lax.broadcasted_iota(jnp.int32, (size, size), 1)
    return (rows + cols == size - 1).astype(F32).astype(BF16)


def kernel(
    ns, nc, nu,
    q_hbm, k_hbm, v_hbm, w_hbm, og_hbm,
    rc, g2,
    q_v, k_v, v_v, w_v, og_v,
    xa, ra, sd, mb, rb, fs, f1, f1s, f2,
    tt, xf, xz0, xz8, gb, gjf, glt, lhs, acc, yst,
    lhe, xd, rd, mc, fgm, fgo, fgt, g1, g1s,
    in_sem, a_send, a_recv, b_send, b_recv, f_send, f_recv,
    d_send, d_recv, c_send, c_recv, g_send, g_recv, h_send, h_recv,
):
    me_s, me_c = lax.axis_index("seq"), lax.axis_index("ch")
    ny = ns // nu
    me_y, me_u = me_s // nu, lax.rem(me_s, nu)
    pr = ns // PARTS
    nb = ns * TB // BLK
    rows = nb * nc
    msg = 2 * nc
    norm = float((ns * TB) ** -0.5)
    lags = min(LAGS, nb)
    my_part = me_s // pr
    nq = nc // 2
    me_p, me_q = me_c // nq, lax.rem(me_c, nq)

    def copy_in(i, src, dst):
        return pltpu.make_async_copy(src, dst, in_sem.at[i])

    loads = [
        copy_in(0, k_hbm, k_v),
        copy_in(1, v_hbm, v_v),
        copy_in(2, og_hbm, og_v),
        copy_in(3, q_hbm, q_v),
        copy_in(4, w_hbm.at[pl.ds(pl.multiple_of(me_q * ns, ns), ns)], w_v.at[0]),
        copy_in(5, w_hbm.at[pl.ds(pl.multiple_of((me_q + nq) * ns, ns), ns)], w_v.at[1]),
    ]
    for load in loads:
        load.start()

    barrier = pltpu.get_barrier_semaphore()

    def greet_seq(o, carry):
        pl.semaphore_signal(barrier, inc=1, device_id={"seq": lax.rem(me_s + o, ns)})
        return carry

    def greet_ch(o, carry):
        pl.semaphore_signal(barrier, inc=1, device_id={"ch": lax.rem(me_c + o, nc)})
        return carry

    lax.fori_loop(1, nc, greet_ch, 0)
    lax.fori_loop(1, ns, greet_seq, 0)

    for load in loads:
        load.wait()

    for c in range(nc):
        f, q = c // nq, c % nq
        for m in range(PARTS):
            at = pl.ds(c * ns + m * pr, pr)
            xa[m, q, f] = (k_v[at].astype(F32) * v_v[at].astype(F32)).astype(BF16)
            xa[m, q, 2 + f] = (og_v[at].astype(F32) * q_v[at].astype(F32)).astype(BF16)
    for f in range(2):
        rows_f = w_v[f].astype(F32)
        for y in range(ny):
            fs[(2 * y + f) * nu : (2 * y + f + 1) * nu] = rows_f[y * nu : (y + 1) * nu]

    pl.semaphore_wait(barrier, ns - 1 + nc - 1)

    def tile(ref, i, size):
        return ref.at[pl.ds(pl.multiple_of(i * size, size), size)]

    def start_y(out_ref, in_ref, send_sem, recv_sem):
        size = out_ref.shape[0] // ny
        def push(o, carry):
            y = lax.rem(me_y + o, ny)
            pltpu.make_async_remote_copy(
                tile(out_ref, y, size), tile(in_ref, me_y, size), send_sem.at[0], recv_sem.at[0],
                device_id={"seq": y * nu + me_u},
            ).start()
            return carry

        lax.fori_loop(1, ny, push, 0)
        pltpu.make_async_copy(
            tile(out_ref, me_y, size), tile(in_ref, me_y, size), recv_sem.at[0]
        ).start()

    def turn_y_start_u(in_ref, mid_ref, end_ref, send_sem, recv_sem):
        wait_all(in_ref, recv_sem.at[0])
        size = in_ref.shape[0] // nu
        sets = size // ny
        for u in range(nu):
            for f in range(sets):
                at = u * size + f * ny
                mid_ref[at : at + ny] = in_ref[pl.ds(f * nu + u, ny, stride=sets * nu), :]

        def push(o, carry):
            u = lax.rem(me_u + o, nu)
            pltpu.make_async_remote_copy(
                tile(mid_ref, u, size), tile(end_ref, me_u, size), send_sem.at[1], recv_sem.at[1],
                device_id={"seq": me_y * nu + u},
            ).start()
            return carry

        lax.fori_loop(1, nu, push, 0)
        pltpu.make_async_copy(
            tile(mid_ref, me_u, size), tile(end_ref, me_u, size), recv_sem.at[1]
        ).start()

    def start_ch(out_ref, in_ref, send_sem, recv_sem):
        for kappa in ORDER:
            m = lax.rem(my_part + kappa, PARTS)

            def push(o, carry):
                q = lax.rem(me_q + o, nq)
                pltpu.make_async_remote_copy(
                    out_ref.at[m, q], in_ref.at[m, me_q], send_sem, recv_sem.at[kappa],
                    device_id={"ch": me_p * nq + q},
                ).start()
                return carry

            lax.fori_loop(1, nq, push, 0)
            pltpu.make_async_copy(out_ref.at[m, me_q], in_ref.at[m, me_q], recv_sem.at[kappa]).start()

    def turn_part(kappa, in_ref, mid_ref, recv_sem):
        m = lax.rem(my_part + kappa, PARTS)
        wait_all(in_ref.at[m], recv_sem.at[kappa])
        for q in range(nq):
            for kind in range(4):
                at = (kind * nq + q) * pr
                sd[at : at + pr] = in_ref[m, q, kind].astype(F32)
        for i in range(pr):
            mid_ref[kappa, i] = sd[pl.ds(i, msg, stride=pr), :].astype(BF16)

    def start_seq_part(kappa, mid_ref, end_ref, send_sem, recv_sem):
        m = lax.rem(my_part + kappa, PARTS)
        mine = lax.rem(me_s, pr)

        def push(o, carry):
            i = lax.rem(mine + o, pr)
            pltpu.make_async_remote_copy(
                mid_ref.at[kappa, i], end_ref.at[me_s], send_sem, recv_sem,
                device_id={"seq": m * pr + i},
            ).start()
            return carry

        lax.fori_loop(1 if kappa == 0 else 0, pr, push, 0)
        if kappa == 0:
            pltpu.make_async_copy(mid_ref.at[kappa, mine], end_ref.at[me_s], recv_sem).start()

    def wait_all(ref, sem):
        pltpu.make_async_copy(ref, ref, sem).wait()

    start_y(fs, f1, f_send, f_recv)
    start_ch(xa, ra, a_send, a_recv)
    turn_y_start_u(f1, f1s, f2, f_send, f_recv)
    for kappa in ORDER:
        turn_part(kappa, ra, mb, a_recv)
        start_seq_part(kappa, mb, rb, b_send, b_recv)

    sub = lax.broadcasted_iota(jnp.int32, (TB, TB), 0)
    lane = lax.broadcasted_iota(jnp.int32, (TB, TB), 1)
    keep = lane >= sub
    zero = jnp.zeros((TB, TB), F32)
    flip = reversal(BLK)
    wait_all(f2, f_recv.at[1])

    def skewed(tile):
        return pltpu.roll(tile, 0, 1, stride=1, stride_axis=0)

    def filter_row(f, s):
        at = (s % nu * 2 + f) * ny + s // nu
        return jnp.broadcast_to(f2[pl.ds(at, 1), :], (TB, TB))

    for f in range(2):
        tt[f, TB:BLK, 0:TB] = zero.astype(BF16)
        before = zero
        for d in range(nb):
            even, odd = skewed(filter_row(f, 2 * d)), skewed(filter_row(f, 2 * d + 1))
            block = jnp.where(keep, even, before).astype(BF16)
            tt[f, d * BLK : d * BLK + TB, 0:TB] = block
            tt[f, d * BLK + TB : (d + 1) * BLK, TB:BLK] = block
            block = jnp.where(keep, odd, even).astype(BF16)
            tt[f, d * BLK : d * BLK + TB, TB:BLK] = block
            tt[f, (d + 1) * BLK + TB : (d + 2) * BLK, 0:TB] = block
            before = odd

    lhs[:, 0 : lags * nc] = jnp.zeros((2, lags * nc, BLK), F32)
    xf[0:rows] = jnp.zeros((rows, BLK), F32)
    xf[2 * rows :] = jnp.zeros((nc, BLK), F32)

    wait_all(rb, b_recv)
    for j in range(nb):
        low, high = rb[2 * j].astype(F32), rb[2 * j + 1].astype(F32)
        xf[rows + j * nc : rows + (j + 1) * nc, 0:TB] = low[0:nc]
        xf[rows + j * nc : rows + (j + 1) * nc, TB:BLK] = high[0:nc]
        gjf[j * nc : (j + 1) * nc, 0:TB] = low[nc:msg]
        gjf[j * nc : (j + 1) * nc, TB:BLK] = high[nc:msg]
    gb[...] = gjf[...].astype(BF16)
    gjf[...] = dot(gb[...], flip)
    first_half = lax.broadcasted_iota(jnp.int32, (nc, BLK), 0) < nq

    def swap(rows_nc):
        return pltpu.roll(rows_nc, nq, 0)

    for j in range(nb):
        back = nb - 1 - j
        x_rows = xf[rows + j * nc : rows + (j + 1) * nc]
        g_rows = gjf[back * nc : (back + 1) * nc]
        at = pl.ds((lags + j) * nc, nc)
        lhs[0, at] = jnp.where(first_half, x_rows, swap(g_rows))
        lhs[1, at] = jnp.where(first_half, swap(x_rows), g_rows)
    for f in range(2):
        for e in range(lags):
            lhe[f, e] = lhs[f, pl.ds((lags - e) * nc, rows)].astype(BF16)

    for f in range(2):
        for first in range(0, nb, lags):
            count = (nb - first) * nc
            left = jnp.concatenate([lhe[f, e, 0:count] for e in range(lags)], axis=1)
            prod = dot(left, tt[f, first * BLK : (first + lags) * BLK])
            if first == 0:
                acc[f] = prod
            else:
                acc[f, first * nc :] += prod

    for j in range(nb):
        back = nb - 1 - j
        zeroth, other = acc[0, pl.ds(j * nc, nc)] * norm, acc[1, pl.ds(j * nc, nc)] * norm
        out = jnp.where(first_half, zeroth, swap(other))
        yst[2 * j * msg : 2 * j * msg + nc] = out[:, 0:TB]
        yst[(2 * j + 1) * msg : (2 * j + 1) * msg + nc] = out[:, TB:BLK]
        gjf[back * nc : (back + 1) * nc] = jnp.where(first_half, swap(zeroth), other)
    gjf[...] = dot(gjf[...].astype(BF16), flip)
    for j in range(nb):
        out = gjf[j * nc : (j + 1) * nc]
        yst[2 * j * msg + nc : (2 * j + 1) * msg] = out[:, 0:TB]
        yst[(2 * j + 1) * msg + nc : (2 * j + 2) * msg] = out[:, TB:BLK]

    for m in range(PARTS):
        for q in range(nq):
            for kind in range(4):
                begin = m * pr * msg + kind * nq + q
                xd[m, q, kind] = yst[pl.ds(begin, pr, stride=msg), :].astype(BF16)
    start_ch(xd, rd, d_send, d_recv)

    turned_g = dot(flip, gb[...], ((1,), (1,)))
    column = lax.rem(lax.broadcasted_iota(jnp.int32, (BLK, rows), 1), nc)
    glt[0:BLK] = jnp.where(column < nq, turned_g, 0.0).astype(BF16)
    glt[BLK:] = jnp.where(column < nq, 0.0, turned_g).astype(BF16)
    xz0[...] = xf[0 : 2 * rows].astype(BF16)
    xz8[...] = xf[nc : 2 * rows + nc].astype(BF16)
    over, before = [zero, zero], [zero, zero]
    for i in range(nb):
        low = (i // 2) * msg
        shifted = xz0[low + msg : low + msg + rows] if i % 2 else xz8[low : low + rows]
        both = dot(glt[...], shifted)
        for f in range(2):
            prod = both[f * BLK : (f + 1) * BLK]
            pair = (prod[0:TB, 0:TB] + over[f], prod[0:TB, TB:BLK] + prod[TB:BLK, 0:TB])
            for half, total in enumerate(pair):
                at = ns - 1 - (2 * i + half)
                turned = skewed(total)
                summed = jnp.sum(jnp.where(keep, turned, before[f]), axis=0, keepdims=True)
                fgm[f, at : at + 1] = summed
                before[f] = turned
            over[f] = prod[TB:BLK, TB:BLK]
    swapped = pltpu.make_async_remote_copy(
        fgm.at[1 - me_p], fgo, h_send, h_recv, device_id={"ch": (1 - me_p) * nq + me_q}
    )
    swapped.start()

    for kappa in ORDER:
        turn_part(kappa, rd, mc, d_recv)
        start_seq_part(kappa, mc, rc, c_send, c_recv)
    swapped.wait()
    fgt[...] = dot(((fgm[me_p] + fgo[...]) * norm).astype(BF16), reversal(TB))
    start_y(fgt, g1, g_send, g_recv)
    turn_y_start_u(g1, g1s, g2, g_send, g_recv)

    wait_all(rc, c_recv)
    wait_all(g2, g_recv.at[1])
    if nq > 1:
        wait_all(xa.at[:, pl.ds(0, nq - 1)], a_send)
        wait_all(xd.at[:, pl.ds(0, nq - 1)], d_send)
    for ref, sem in ((rb, b_send), (rc, c_send)):
        wait_all(ref.at[pl.ds(0, ns - 1)], sem)
    for ref, sem in ((f1, f_send), (g1, g_send)):
        size = ref.shape[0]
        wait_all(ref.at[pl.ds(0, size - size // ny)], sem.at[0])
        wait_all(ref.at[pl.ds(0, size - size // nu)], sem.at[1])


def finish(ns, nc, nu, rc, g2, k_v, v_v, og_v, qg_out, kg_out, vg_out, fg_out, rcf):
    msg, ny = 2 * nc, ns // nu
    rcf[...] = rc[...].astype(F32).reshape(ns * msg, TB)
    for c in range(nc):
        at = pl.ds(c * ns, ns)
        conv = rcf[pl.ds(c, ns, stride=msg), :]
        grad = rcf[pl.ds(nc + c, ns, stride=msg), :]
        qg_out[at] = (og_v[at].astype(F32) * conv).astype(BF16)
        kg_out[at] = (grad * v_v[at].astype(F32)).astype(BF16)
        vg_out[at] = (grad * k_v[at].astype(F32)).astype(BF16)
    for y in range(0, ny, 2):
        two = [g2[pl.ds(y + i, nu, stride=ny), :] for i in range(2)]
        fg_out[y * nu : (y + 2) * nu] = jnp.concatenate(two, axis=0).astype(BF16)


def shards(ns, nc, query_gate, key_gate, value_in, filter_weight, output_grad):
    local = query_gate.shape[0]
    nb, nu = ns * TB // BLK, math.isqrt(ns)
    ny = ns // nu
    rows, msg, pr = nb * nc, 2 * nc, ns // PARTS
    nq, lags = nc // 2, min(LAGS, nb)
    bf, f32 = (lambda *shape: pltpu.VMEM(shape, BF16)), (lambda *shape: pltpu.VMEM(shape, F32))
    one = pltpu.SemaphoreType.DMA(())
    two = pltpu.SemaphoreType.DMA((2,))
    some = pltpu.SemaphoreType.DMA((PARTS,))
    any_spec = pl.BlockSpec(memory_space=pl.ANY)
    vmem_spec = pl.BlockSpec(memory_space=pltpu.VMEM)
    moved, filter_part = pl.pallas_call(
        functools.partial(kernel, ns, nc, nu),
        out_shape=(
            jax.ShapeDtypeStruct((ns, msg, TB), BF16),
            jax.ShapeDtypeStruct((ns, TB), F32),
        ),
        in_specs=[any_spec] * 5,
        out_specs=(any_spec,) * 2,
        scratch_shapes=[
            bf(local, TB), bf(local, TB), bf(local, TB), bf(2, ns, TB), bf(local, TB),
            bf(PARTS, nq, 4, pr, TB), bf(PARTS, nq, 4, pr, TB), f32(msg * pr, TB),
            bf(PARTS, pr, msg, TB), bf(ns, msg, TB),
            f32(2 * ns, TB), f32(2 * ns, TB), f32(2 * ns, TB), f32(2 * ns, TB),
            bf(2, (nb + 1) * BLK, BLK), f32(2 * rows + nc, BLK), bf(2 * rows, BLK), bf(2 * rows, BLK),
            bf(rows, BLK), f32(rows, BLK), bf(2 * BLK, rows), f32(2, (lags + nb) * nc, BLK),
            f32(2, rows, BLK), f32(ns * msg, TB), bf(2, lags, rows, BLK),
            bf(PARTS, nq, 4, pr, TB), bf(PARTS, nq, 4, pr, TB),
            bf(PARTS, pr, msg, TB), f32(2, ns, TB), f32(ns, TB), f32(ns, TB), f32(ns, TB), f32(ns, TB),
            pltpu.SemaphoreType.DMA((6,)), one, some, one, one, two, two,
            one, some, one, one, two, two, one, one,
        ],
        compiler_params=pltpu.CompilerParams(
            collective_id=0, has_side_effects=True, vmem_limit_bytes=VMEM_BYTES
        ),
    )(query_gate, key_gate, value_in, filter_weight, output_grad)
    wide = jax.ShapeDtypeStruct((local, TB), BF16)
    return pl.pallas_call(
        functools.partial(finish, ns, nc, nu),
        out_shape=(wide, wide, wide, jax.ShapeDtypeStruct((ns, TB), BF16)),
        in_specs=[vmem_spec] * 5,
        out_specs=(vmem_spec,) * 4,
        scratch_shapes=[f32(ns * msg, TB)],
        compiler_params=pltpu.CompilerParams(vmem_limit_bytes=VMEM_BYTES),
    )(moved, filter_part, key_gate, value_in, output_grad)


def solution(mesh):
    ns, nc = mesh.shape["seq"], mesh.shape["ch"]
    placed = (P("ch", "seq"), P("ch", "seq"), P("ch", "seq"), P(None, "seq"), P("ch", "seq"))
    return jax.shard_map(
        functools.partial(shards, ns, nc),
        mesh=mesh,
        in_specs=placed,
        out_specs=(P("ch", "seq"),) * 4,
        check_vma=False,
    )
```

time: 54.5 us -> 58.6 us (1.075); the launches traced: 54.3 us -> 57.6 us
  Pallas kernels: 53.7 us -> 57 us
    pallas_call x1, Pallas kernels: 51.6 us -> 54.9 us  [shards(): pl.pallas_call(functools.partial(kernel, ns, nc, nu), out_shape=(jax.Shap...]
where the time goes in v3:
time: 58.6 us; the launch traced here: 57.6 us
  Pallas kernels  57 us (97%)
  between operations  0.64 us (1%)
    pallas_call x1, Pallas kernels, shards(): pl.pallas_call(functools.partial(kernel, ns, nc, nu), out_shape=(jax.Shap...  54.9 us
    pallas_call x1, Pallas kernels, shards(): pl.pallas_call(functools.partial(finish, ns, nc, nu), out_shape=(wide, wi...  2.09 us

profile of v3, /device:TPU:1, one launch (start us, length us, event | category | flops | bytes accessed | tf_op | source)
XLA Modules:
  0.0 57.6 jit_solution(75378685255569839)
XLA Ops:
  0.6 54.9 %shard_map.84 = (bf16[64,16,128]{2,1,0:T(8,128)(2,1)}, f32[64,128]{1,0:T(8,128)}) custom-call(bf16[512,128]{1,0:T(8,128)(2,1)} %q_hbm.1, bf16[512,128]{1,0:T(8,128)(2,1)} %k_v.1, bf16[512,128]{1,0:T(8,128)(2,1)} %v_v.1, bf16[512,128]{1,0:T(8,128)(2,1)} %w_hbm.1, bf16[512,128]{1,0:T(8,128)(2,1)} %og_v.1), custom_call_target="tpu_custom_call" | custom-call | tf_op jit(solution)/shard_map/pallas_call | solution.py:349
  55.5 2.1 %shard_map.85 = (bf16[512,128]{1,0:T(8,128)(2,1)}, bf16[512,128]{1,0:T(8,128)(2,1)}, bf16[512,128]{1,0:T(8,128)(2,1)}, bf16[64,128]{1,0:T(8,128)(2,1)}) custom-call(bf16[64,16,128]{2,1,0:T(8,128)(2,1)} %get-tuple-element.6.rc, f32[64,128]{1,0:T(8,128)} %get-tuple-element.7.g2, bf16[512,128]{1,0:T(8,128)(2,1)} %k_v.1, bf16[512,128]{1,0:T(8,128)(2,1)} %v_v.1, ...), custom_call_target="tpu_custom_call" | custom-call | tf_op jit(solution)/shard_map/pallas_call | solution.py:375

commit v4 on v3

--- a/solution.py
+++ b/solution.py
@@ -35,9 +35,9 @@
     q_v, k_v, v_v, w_v, og_v,
     xa, ra, sd, mb, rb, fs, f1, f1s, f2,
     tt, xf, xz0, xz8, gb, gjf, glt, lhs, acc, yst,
-    lhe, xd, rd, mc, fgm, fgo, fgt, g1, g1s,
+    lhe, xd, rd, mc, fgm, fgt, g1, g1s,
     in_sem, a_send, a_recv, b_send, b_recv, f_send, f_recv,
-    d_send, d_recv, c_send, c_recv, g_send, g_recv, h_send, h_recv,
+    d_send, d_recv, c_send, c_recv, g_send, g_recv, h_send, h_recv, ready,
 ):
     me_s, me_c = lax.axis_index("seq"), lax.axis_index("ch")
     ny = ns // nu
@@ -72,12 +72,18 @@
         pl.semaphore_signal(barrier, inc=1, device_id={"seq": lax.rem(me_s + o, ns)})
         return carry
 
-    def greet_ch(o, carry):
-        pl.semaphore_signal(barrier, inc=1, device_id={"ch": lax.rem(me_c + o, nc)})
-        return carry
-
-    lax.fori_loop(1, nc, greet_ch, 0)
+    def partner(y):
+        return {"seq": y * nu + me_u, "ch": (1 - me_p) * nq + me_q}
+
+    for o in range(1, nq):
+        member = {"ch": me_p * nq + lax.rem(me_q + o, nq)}
+        pl.semaphore_signal(barrier, inc=1, device_id=member)
     lax.fori_loop(1, ns, greet_seq, 0)
+
+    @pl.when(me_p == 0)
+    def _():
+        for y in range(ny):
+            pl.semaphore_signal(barrier, inc=1, device_id=partner(y))
 
     for load in loads:
         load.wait()
@@ -93,28 +99,31 @@
         for y in range(ny):
             fs[(2 * y + f) * nu : (2 * y + f + 1) * nu] = rows_f[y * nu : (y + 1) * nu]
 
-    pl.semaphore_wait(barrier, ns - 1 + nc - 1)
+    pl.semaphore_wait(barrier, ns - 1 + nq - 1 + me_p * ny)
+
+    @pl.when(me_p == 1)
+    def _():
+        for y in range(ny):
+            pl.semaphore_signal(ready, inc=1, device_id=partner(y))
 
     def tile(ref, i, size):
         return ref.at[pl.ds(pl.multiple_of(i * size, size), size)]
 
     def start_y(out_ref, in_ref, send_sem, recv_sem):
         size = out_ref.shape[0] // ny
+
         def push(o, carry):
             y = lax.rem(me_y + o, ny)
             pltpu.make_async_remote_copy(
-                tile(out_ref, y, size), tile(in_ref, me_y, size), send_sem.at[0], recv_sem.at[0],
+                tile(out_ref, y, size), tile(in_ref, me_y, size), send_sem, recv_sem,
                 device_id={"seq": y * nu + me_u},
             ).start()
             return carry
 
         lax.fori_loop(1, ny, push, 0)
-        pltpu.make_async_copy(
-            tile(out_ref, me_y, size), tile(in_ref, me_y, size), recv_sem.at[0]
-        ).start()
+        pltpu.make_async_copy(tile(out_ref, me_y, size), tile(in_ref, me_y, size), recv_sem).start()
 
     def turn_y_start_u(in_ref, mid_ref, end_ref, send_sem, recv_sem):
-        wait_all(in_ref, recv_sem.at[0])
         size = in_ref.shape[0] // nu
         sets = size // ny
         for u in range(nu):
@@ -125,15 +134,13 @@
         def push(o, carry):
             u = lax.rem(me_u + o, nu)
             pltpu.make_async_remote_copy(
-                tile(mid_ref, u, size), tile(end_ref, me_u, size), send_sem.at[1], recv_sem.at[1],
+                tile(mid_ref, u, size), tile(end_ref, me_u, size), send_sem, recv_sem,
                 device_id={"seq": me_y * nu + u},
             ).start()
             return carry
 
         lax.fori_loop(1, nu, push, 0)
-        pltpu.make_async_copy(
-            tile(mid_ref, me_u, size), tile(end_ref, me_u, size), recv_sem.at[1]
-        ).start()
+        pltpu.make_async_copy(tile(mid_ref, me_u, size), tile(end_ref, me_u, size), recv_sem).start()
 
     def start_ch(out_ref, in_ref, send_sem, recv_sem):
         for kappa in ORDER:
@@ -179,9 +186,10 @@
     def wait_all(ref, sem):
         pltpu.make_async_copy(ref, ref, sem).wait()
 
-    start_y(fs, f1, f_send, f_recv)
+    start_y(fs, f1, f_send.at[0], f_recv.at[0])
     start_ch(xa, ra, a_send, a_recv)
-    turn_y_start_u(f1, f1s, f2, f_send, f_recv)
+    wait_all(f1, f_recv.at[0])
+    turn_y_start_u(f1, f1s, f2, f_send.at[1], f_recv.at[1])
     for kappa in ORDER:
         turn_part(kappa, ra, mb, a_recv)
         start_seq_part(kappa, mb, rb, b_send, b_recv)
@@ -230,47 +238,6 @@
 
     def swap(rows_nc):
         return pltpu.roll(rows_nc, nq, 0)
-
-    for j in range(nb):
-        back = nb - 1 - j
-        x_rows = xf[rows + j * nc : rows + (j + 1) * nc]
-        g_rows = gjf[back * nc : (back + 1) * nc]
-        at = pl.ds((lags + j) * nc, nc)
-        lhs[0, at] = jnp.where(first_half, x_rows, swap(g_rows))
-        lhs[1, at] = jnp.where(first_half, swap(x_rows), g_rows)
-    for f in range(2):
-        for e in range(lags):
-            lhe[f, e] = lhs[f, pl.ds((lags - e) * nc, rows)].astype(BF16)
-
-    for f in range(2):
-        for first in range(0, nb, lags):
-            count = (nb - first) * nc
-            left = jnp.concatenate([lhe[f, e, 0:count] for e in range(lags)], axis=1)
-            prod = dot(left, tt[f, first * BLK : (first + lags) * BLK])
-            if first == 0:
-                acc[f] = prod
-            else:
-                acc[f, first * nc :] += prod
-
-    for j in range(nb):
-        back = nb - 1 - j
-        zeroth, other = acc[0, pl.ds(j * nc, nc)] * norm, acc[1, pl.ds(j * nc, nc)] * norm
-        out = jnp.where(first_half, zeroth, swap(other))
-        yst[2 * j * msg : 2 * j * msg + nc] = out[:, 0:TB]
-        yst[(2 * j + 1) * msg : (2 * j + 1) * msg + nc] = out[:, TB:BLK]
-        gjf[back * nc : (back + 1) * nc] = jnp.where(first_half, swap(zeroth), other)
-    gjf[...] = dot(gjf[...].astype(BF16), flip)
-    for j in range(nb):
-        out = gjf[j * nc : (j + 1) * nc]
-        yst[2 * j * msg + nc : (2 * j + 1) * msg] = out[:, 0:TB]
-        yst[(2 * j + 1) * msg + nc : (2 * j + 2) * msg] = out[:, TB:BLK]
-
-    for m in range(PARTS):
-        for q in range(nq):
-            for kind in range(4):
-                begin = m * pr * msg + kind * nq + q
-                xd[m, q, kind] = yst[pl.ds(begin, pr, stride=msg), :].astype(BF16)
-    start_ch(xd, rd, d_send, d_recv)
 
     turned_g = dot(flip, gb[...], ((1,), (1,)))
     column = lax.rem(lax.broadcasted_iota(jnp.int32, (BLK, rows), 1), nc)
@@ -293,18 +260,72 @@
                 fgm[f, at : at + 1] = summed
                 before[f] = turned
             over[f] = prod[TB:BLK, TB:BLK]
-    swapped = pltpu.make_async_remote_copy(
-        fgm.at[1 - me_p], fgo, h_send, h_recv, device_id={"ch": (1 - me_p) * nq + me_q}
-    )
-    swapped.start()
-
-    for kappa in ORDER:
-        turn_part(kappa, rd, mc, d_recv)
-        start_seq_part(kappa, mc, rc, c_send, c_recv)
-    swapped.wait()
-    fgt[...] = dot(((fgm[me_p] + fgo[...]) * norm).astype(BF16), reversal(TB))
-    start_y(fgt, g1, g_send, g_recv)
-    turn_y_start_u(g1, g1s, g2, g_send, g_recv)
+    start_y(fgm.at[me_p], g1.at[0], g_send.at[0], g_recv.at[0])
+
+    @pl.when(me_p == 0)
+    def _():
+        pl.semaphore_wait(ready, ny)
+
+    def push_other(o, carry):
+        y = lax.rem(me_y + o, ny)
+        pltpu.make_async_remote_copy(
+            tile(fgm.at[1 - me_p], y, nu), tile(g1.at[1], me_y, nu), h_send, h_recv,
+            device_id=partner(y),
+        ).start()
+        return carry
+
+    lax.fori_loop(0, ny, push_other, 0)
+
+    for j in range(nb):
+        back = nb - 1 - j
+        x_rows = xf[rows + j * nc : rows + (j + 1) * nc]
+        g_rows = gjf[back * nc : (back + 1) * nc]
+        at = pl.ds((lags + j) * nc, nc)
+        lhs[0, at] = jnp.where(first_half, x_rows, swap(g_rows))
+        lhs[1, at] = jnp.where(first_half, swap(x_rows), g_rows)
+    for f in range(2):
+        for e in range(lags):
+            lhe[f, e] = lhs[f, pl.ds((lags - e) * nc, rows)].astype(BF16)
+
+    for f in range(2):
+        for first in range(0, nb, lags):
+            count = (nb - first) * nc
+            left = jnp.concatenate([lhe[f, e, 0:count] for e in range(lags)], axis=1)
+            prod = dot(left, tt[f, first * BLK : (first + lags) * BLK])
+            if first == 0:
+                acc[f] = prod
+            else:
+                acc[f, first * nc :] += prod
+
+    for j in range(nb):
+        back = nb - 1 - j
+        zeroth, other = acc[0, pl.ds(j * nc, nc)] * norm, acc[1, pl.ds(j * nc, nc)] * norm
+        out = jnp.where(first_half, zeroth, swap(other))
+        yst[2 * j * msg : 2 * j * msg + nc] = out[:, 0:TB]
+        yst[(2 * j + 1) * msg : (2 * j + 1) * msg + nc] = out[:, TB:BLK]
+        gjf[back * nc : (back + 1) * nc] = jnp.where(first_half, swap(zeroth), other)
+    gjf[...] = dot(gjf[...].astype(BF16), flip)
+    for j in range(nb):
+        out = gjf[j * nc : (j + 1) * nc]
+        yst[2 * j * msg + nc : (2 * j + 1) * msg] = out[:, 0:TB]
+        yst[(2 * j + 1) * msg + nc : (2 * j + 2) * msg] = out[:, TB:BLK]
+
+    for m in range(PARTS):
+        for q in range(nq):
+            for kind in range(4):
+                begin = m * pr * msg + kind * nq + q
+                xd[m, q, kind] = yst[pl.ds(begin, pr, stride=msg), :].astype(BF16)
+    start_ch(xd, rd, d_send, d_recv)
+
+    for step, kappa in enumerate(ORDER + (None,)):
+        if step == 2:
+            wait_all(g1.at[0], g_recv.at[0])
+            wait_all(g1.at[1], h_recv)
+            fgt[...] = dot(((g1[0] + g1[1]) * norm).astype(BF16), reversal(TB))
+            turn_y_start_u(fgt, g1s, g2, g_send.at[1], g_recv.at[1])
+        if kappa is not None:
+            turn_part(kappa, rd, mc, d_recv)
+            start_seq_part(kappa, mc, rc, c_send, c_recv)
 
     wait_all(rc, c_recv)
     wait_all(g2, g_recv.at[1])
@@ -313,7 +334,8 @@
         wait_all(xd.at[:, pl.ds(0, nq - 1)], d_send)
     for ref, sem in ((rb, b_send), (rc, c_send)):
         wait_all(ref.at[pl.ds(0, ns - 1)], sem)
-    for ref, sem in ((f1, f_send), (g1, g_send)):
+    wait_all(g1.at[1], h_send)
+    for ref, sem in ((f1, f_send), (g1s, g_send)):
         size = ref.shape[0]
         wait_all(ref.at[pl.ds(0, size - size // ny)], sem.at[0])
         wait_all(ref.at[pl.ds(0, size - size // nu)], sem.at[1])
@@ -363,9 +385,9 @@
             bf(rows, BLK), f32(rows, BLK), bf(2 * BLK, rows), f32(2, (lags + nb) * nc, BLK),
             f32(2, rows, BLK), f32(ns * msg, TB), bf(2, lags, rows, BLK),
             bf(PARTS, nq, 4, pr, TB), bf(PARTS, nq, 4, pr, TB),
-            bf(PARTS, pr, msg, TB), f32(2, ns, TB), f32(ns, TB), f32(ns, TB), f32(ns, TB), f32(ns, TB),
+            bf(PARTS, pr, msg, TB), f32(2, ns, TB), f32(ns, TB), f32(2, ns, TB), f32(ns, TB),
             pltpu.SemaphoreType.DMA((6,)), one, some, one, one, two, two,
-            one, some, one, one, two, two, one, one,
+            one, some, one, one, two, two, one, one, pltpu.SemaphoreType.REGULAR,
         ],
         compiler_params=pltpu.CompilerParams(
             collective_id=0, has_side_effects=True, vmem_limit_bytes=VMEM_BYTES

time: 58.6 us -> 51.6 us (0.88)
  Pallas kernels: 57 us -> 50.4 us
    pallas_call x1, Pallas kernels: 54.9 us -> 48.3 us  [shards(): pl.pallas_call(functools.partial(kernel, ns, nc, nu), out_shape=(jax.Shap...]
where the time goes in v4:
time: 51.6 us; the launch traced here: 51 us
  Pallas kernels  50.4 us (98%)
  between operations  0.64 us (1%)
    pallas_call x1, Pallas kernels, shards(): pl.pallas_call(functools.partial(kernel, ns, nc, nu), out_shape=(jax.Shap...  48.3 us
    pallas_call x1, Pallas kernels, shards(): pl.pallas_call(functools.partial(finish, ns, nc, nu), out_shape=(wide, wi...  2.09 us

profile of v4, /device:TPU:1, one launch (start us, length us, event | category | flops | bytes accessed | tf_op | source)
XLA Modules:
  0.0 51.0 jit_solution(14125072477018615004)
XLA Ops:
  0.6 48.3 %shard_map.84 = (bf16[64,16,128]{2,1,0:T(8,128)(2,1)}, f32[64,128]{1,0:T(8,128)}) custom-call(bf16[512,128]{1,0:T(8,128)(2,1)} %q_hbm.1, bf16[512,128]{1,0:T(8,128)(2,1)} %k_v.1, bf16[512,128]{1,0:T(8,128)(2,1)} %v_v.1, bf16[512,128]{1,0:T(8,128)(2,1)} %w_hbm.1, bf16[512,128]{1,0:T(8,128)(2,1)} %og_v.1), custom_call_target="tpu_custom_call" | custom-call | tf_op jit(solution)/shard_map/pallas_call | solution.py:371
  48.9 2.1 %shard_map.85 = (bf16[512,128]{1,0:T(8,128)(2,1)}, bf16[512,128]{1,0:T(8,128)(2,1)}, bf16[512,128]{1,0:T(8,128)(2,1)}, bf16[64,128]{1,0:T(8,128)(2,1)}) custom-call(bf16[64,16,128]{2,1,0:T(8,128)(2,1)} %get-tuple-element.6.rc, f32[64,128]{1,0:T(8,128)} %get-tuple-element.7.g2, bf16[512,128]{1,0:T(8,128)(2,1)} %k_v.1, bf16[512,128]{1,0:T(8,128)(2,1)} %v_v.1, ...), custom_call_target="tpu_custom_call" | custom-call | tf_op jit(solution)/shard_map/pallas_call | solution.py:397

commit v5 on v4

--- a/solution.py
+++ b/solution.py
@@ -78,7 +78,8 @@
     for o in range(1, nq):
         member = {"ch": me_p * nq + lax.rem(me_q + o, nq)}
         pl.semaphore_signal(barrier, inc=1, device_id=member)
-    lax.fori_loop(1, ns, greet_seq, 0)
+    for o in range(1, ns):
+        greet_seq(o, 0)
 
     @pl.when(me_p == 0)
     def _():
@@ -186,8 +187,8 @@
     def wait_all(ref, sem):
         pltpu.make_async_copy(ref, ref, sem).wait()
 
+    start_ch(xa, ra, a_send, a_recv)
     start_y(fs, f1, f_send.at[0], f_recv.at[0])
-    start_ch(xa, ra, a_send, a_recv)
     wait_all(f1, f_recv.at[0])
     turn_y_start_u(f1, f1s, f2, f_send.at[1], f_recv.at[1])
     for kappa in ORDER:
@@ -239,42 +240,45 @@
     def swap(rows_nc):
         return pltpu.roll(rows_nc, nq, 0)
 
-    turned_g = dot(flip, gb[...], ((1,), (1,)))
-    column = lax.rem(lax.broadcasted_iota(jnp.int32, (BLK, rows), 1), nc)
-    glt[0:BLK] = jnp.where(column < nq, turned_g, 0.0).astype(BF16)
-    glt[BLK:] = jnp.where(column < nq, 0.0, turned_g).astype(BF16)
-    xz0[...] = xf[0 : 2 * rows].astype(BF16)
-    xz8[...] = xf[nc : 2 * rows + nc].astype(BF16)
-    over, before = [zero, zero], [zero, zero]
-    for i in range(nb):
-        low = (i // 2) * msg
-        shifted = xz0[low + msg : low + msg + rows] if i % 2 else xz8[low : low + rows]
-        both = dot(glt[...], shifted)
-        for f in range(2):
-            prod = both[f * BLK : (f + 1) * BLK]
-            pair = (prod[0:TB, 0:TB] + over[f], prod[0:TB, TB:BLK] + prod[TB:BLK, 0:TB])
-            for half, total in enumerate(pair):
-                at = ns - 1 - (2 * i + half)
-                turned = skewed(total)
-                summed = jnp.sum(jnp.where(keep, turned, before[f]), axis=0, keepdims=True)
-                fgm[f, at : at + 1] = summed
-                before[f] = turned
-            over[f] = prod[TB:BLK, TB:BLK]
-    start_y(fgm.at[me_p], g1.at[0], g_send.at[0], g_recv.at[0])
-
-    @pl.when(me_p == 0)
-    def _():
-        pl.semaphore_wait(ready, ny)
-
-    def push_other(o, carry):
-        y = lax.rem(me_y + o, ny)
-        pltpu.make_async_remote_copy(
-            tile(fgm.at[1 - me_p], y, nu), tile(g1.at[1], me_y, nu), h_send, h_recv,
-            device_id=partner(y),
-        ).start()
-        return carry
-
-    lax.fori_loop(0, ny, push_other, 0)
+    def filter_gradient():
+        turned_g = dot(flip, gb[...], ((1,), (1,)))
+        column = lax.rem(lax.broadcasted_iota(jnp.int32, (BLK, rows), 1), nc)
+        glt[0:BLK] = jnp.where(column < nq, turned_g, 0.0).astype(BF16)
+        glt[BLK:] = jnp.where(column < nq, 0.0, turned_g).astype(BF16)
+        xz0[...] = xf[0 : 2 * rows].astype(BF16)
+        xz8[...] = xf[nc : 2 * rows + nc].astype(BF16)
+        over, before = [zero, zero], [zero, zero]
+        for i in range(nb):
+            low = (i // 2) * msg
+            shifted = xz0[low + msg : low + msg + rows] if i % 2 else xz8[low : low + rows]
+            both = dot(glt[...], shifted)
+            for f in range(2):
+                prod = both[f * BLK : (f + 1) * BLK]
+                pair = (prod[0:TB, 0:TB] + over[f], prod[0:TB, TB:BLK] + prod[TB:BLK, 0:TB])
+                for half, total in enumerate(pair):
+                    at = ns - 1 - (2 * i + half)
+                    turned = skewed(total)
+                    summed = jnp.sum(jnp.where(keep, turned, before[f]), axis=0, keepdims=True)
+                    fgm[f, at : at + 1] = summed
+                    before[f] = turned
+                over[f] = prod[TB:BLK, TB:BLK]
+        start_y(fgm.at[me_p], g1.at[0], g_send.at[0], g_recv.at[0])
+
+        @pl.when(me_p == 0)
+        def _():
+            pl.semaphore_wait(ready, ny)
+
+        def push_other(o, carry):
+            y = lax.rem(me_y + o, ny)
+            pltpu.make_async_remote_copy(
+                tile(fgm.at[1 - me_p], y, nu), tile(g1.at[1], me_y, nu), h_send, h_recv,
+                device_id=partner(y),
+            ).start()
+            return carry
+
+        lax.fori_loop(0, ny, push_other, 0)
+
+    pl.when(me_p == 1)(filter_gradient)
 
     for j in range(nb):
         back = nb - 1 - j
@@ -317,8 +321,10 @@
                 xd[m, q, kind] = yst[pl.ds(begin, pr, stride=msg), :].astype(BF16)
     start_ch(xd, rd, d_send, d_recv)
 
+    pl.when(me_p == 0)(filter_gradient)
+
     for step, kappa in enumerate(ORDER + (None,)):
-        if step == 2:
+        if step == 3:
             wait_all(g1.at[0], g_recv.at[0])
             wait_all(g1.at[1], h_recv)
             fgt[...] = dot(((g1[0] + g1[1]) * norm).astype(BF16), reversal(TB))

time: 51.6 us -> 49.9 us (0.967)
  Pallas kernels: 50.4 us -> 48.4 us
    pallas_call x1, Pallas kernels: 48.3 us -> 46.3 us  [shards(): pl.pallas_call(functools.partial(kernel, ns, nc, nu), out_shape=(jax.Shap...]
where the time goes in v5:
time: 49.9 us; the launch traced here: 49 us
  Pallas kernels  48.4 us (97%)
  between operations  0.64 us (1%)
    pallas_call x1, Pallas kernels, shards(): pl.pallas_call(functools.partial(kernel, ns, nc, nu), out_shape=(jax.Shap...  46.3 us
    pallas_call x1, Pallas kernels, shards(): pl.pallas_call(functools.partial(finish, ns, nc, nu), out_shape=(wide, wi...  2.09 us

profile of v5, /device:TPU:1, one launch (start us, length us, event | category | flops | bytes accessed | tf_op | source)
XLA Modules:
  0.0 49.0 jit_solution(7175660631794680917)
XLA Ops:
  0.6 46.3 %shard_map.84 = (bf16[64,16,128]{2,1,0:T(8,128)(2,1)}, f32[64,128]{1,0:T(8,128)}) custom-call(bf16[512,128]{1,0:T(8,128)(2,1)} %q_hbm.1, bf16[512,128]{1,0:T(8,128)(2,1)} %k_v.1, bf16[512,128]{1,0:T(8,128)(2,1)} %v_v.1, bf16[512,128]{1,0:T(8,128)(2,1)} %w_hbm.1, bf16[512,128]{1,0:T(8,128)(2,1)} %og_v.1), custom_call_target="tpu_custom_call" | custom-call | tf_op jit(solution)/shard_map/pallas_call | solution.py:377
  46.9 2.1 %shard_map.85 = (bf16[512,128]{1,0:T(8,128)(2,1)}, bf16[512,128]{1,0:T(8,128)(2,1)}, bf16[512,128]{1,0:T(8,128)(2,1)}, bf16[64,128]{1,0:T(8,128)(2,1)}) custom-call(bf16[64,16,128]{2,1,0:T(8,128)(2,1)} %get-tuple-element.6.rc, f32[64,128]{1,0:T(8,128)} %get-tuple-element.7.g2, bf16[512,128]{1,0:T(8,128)(2,1)} %k_v.1, bf16[512,128]{1,0:T(8,128)(2,1)} %v_v.1, ...), custom_call_target="tpu_custom_call" | custom-call | tf_op jit(solution)/shard_map/pallas_call | solution.py:403

commit v6 on v5

--- a/solution.py
+++ b/solution.py
@@ -143,19 +143,22 @@
         lax.fori_loop(1, nu, push, 0)
         pltpu.make_async_copy(tile(mid_ref, me_u, size), tile(end_ref, me_u, size), recv_sem).start()
 
+    others = [lax.rem(me_q + o, nq) for o in range(1, nq)]
+    if nq == 4:
+        others = [nq - 1 - me_q, lax.rem(me_q + 2, nq), me_q + 1 - 2 * lax.rem(me_q, 2)]
+
     def start_ch(out_ref, in_ref, send_sem, recv_sem):
         for kappa in ORDER:
             m = lax.rem(my_part + kappa, PARTS)
 
-            def push(o, carry):
-                q = lax.rem(me_q + o, nq)
+            def push(q):
                 pltpu.make_async_remote_copy(
                     out_ref.at[m, q], in_ref.at[m, me_q], send_sem, recv_sem.at[kappa],
                     device_id={"ch": me_p * nq + q},
                 ).start()
-                return carry
-
-            lax.fori_loop(1, nq, push, 0)
+
+            for q in others:
+                push(q)
             pltpu.make_async_copy(out_ref.at[m, me_q], in_ref.at[m, me_q], recv_sem.at[kappa]).start()
 
     def turn_part(kappa, in_ref, mid_ref, recv_sem):
@@ -180,7 +183,8 @@
             ).start()
             return carry
 
-        lax.fori_loop(1 if kappa == 0 else 0, pr, push, 0)
+        for o in range(1 if kappa == 0 else 0, pr):
+            push(o, 0)
         if kappa == 0:
             pltpu.make_async_copy(mid_ref.at[kappa, mine], end_ref.at[me_s], recv_sem).start()
 

time: 49.9 us -> 49.4 us (0.990)
  Pallas kernels: 48.4 us -> 47.9 us
where the time goes in v6:
time: 49.4 us; the launch traced here: 48.5 us
  Pallas kernels  47.9 us (97%)
  between operations  0.64 us (1%)
    pallas_call x1, Pallas kernels, shards(): pl.pallas_call(functools.partial(kernel, ns, nc, nu), out_shape=(jax.Shap...  45.8 us
    pallas_call x1, Pallas kernels, shards(): pl.pallas_call(functools.partial(finish, ns, nc, nu), out_shape=(wide, wi...  2.09 us

profile of v6, /device:TPU:1, one launch (start us, length us, event | category | flops | bytes accessed | tf_op | source)
XLA Modules:
  0.0 48.5 jit_solution(17931783964862912120)
XLA Ops:
  0.6 45.8 %shard_map.84 = (bf16[64,16,128]{2,1,0:T(8,128)(2,1)}, f32[64,128]{1,0:T(8,128)}) custom-call(bf16[512,128]{1,0:T(8,128)(2,1)} %q_hbm.1, bf16[512,128]{1,0:T(8,128)(2,1)} %k_v.1, bf16[512,128]{1,0:T(8,128)(2,1)} %v_v.1, bf16[512,128]{1,0:T(8,128)(2,1)} %w_hbm.1, bf16[512,128]{1,0:T(8,128)(2,1)} %og_v.1), custom_call_target="tpu_custom_call" | custom-call | tf_op jit(solution)/shard_map/pallas_call | solution.py:381
  46.5 2.1 %shard_map.85 = (bf16[512,128]{1,0:T(8,128)(2,1)}, bf16[512,128]{1,0:T(8,128)(2,1)}, bf16[512,128]{1,0:T(8,128)(2,1)}, bf16[64,128]{1,0:T(8,128)(2,1)}) custom-call(bf16[64,16,128]{2,1,0:T(8,128)(2,1)} %get-tuple-element.6.rc, f32[64,128]{1,0:T(8,128)} %get-tuple-element.7.g2, bf16[512,128]{1,0:T(8,128)(2,1)} %k_v.1, bf16[512,128]{1,0:T(8,128)(2,1)} %v_v.1, ...), custom_call_target="tpu_custom_call" | custom-call | tf_op jit(solution)/shard_map/pallas_call | solution.py:407
